TPU v7x, 32 devices: a whole 2x2x4 slice. The times are simulated.
32 devices in a mesh: lat: 4 (over y, x), lon: 8 (over z, core).
Axes of the slice: x: 2, y: 2, z: 4, core: 2. Of those that a mesh axis runs over, the one named last changes fastest.
Arguments:
- tokens: bfloat16 [48, 384, 512], P('lat', 'lon'), may hold values from -6 to 6
- fine_qkv: bfloat16 [512, 1536], replicated, may hold values from -12 to 12
- fine_out: bfloat16 [512, 512], replicated, may hold values from -0.25 to 0.25
- fine_up: bfloat16 [512, 2048], replicated, may hold values from -0.25 to 0.25
- fine_down: bfloat16 [2048, 512], replicated, may hold values from -0.125 to 0.125
- merge_weight: bfloat16 [2048, 1024], replicated, may hold values from -0.125 to 0.125
- coarse_qkv: bfloat16 [1024, 3072], P(None, 'lon'), may hold values from -12 to 12
- coarse_out: bfloat16 [1024, 1024], P(None, 'lon'), may hold values from -0.1875 to 0.1875
- coarse_up: bfloat16 [1024, 4096], P(None, 'lon'), may hold values from -0.1875 to 0.1875
- coarse_down: bfloat16 [1024, 4096], P(None, 'lon'), may hold values from -0.09375 to 0.09375
- split_weight: bfloat16 [1024, 2048], replicated, may hold values from -0.1875 to 0.1875
Outputs:
- fine_result: bfloat16 [48, 384, 512], P('lat', 'lon')
All inputs are finite; a program needn't handle non-finite values.
Results may differ from a plain program's by a relative error of at most 0.014.
Values may be sent and summed in bfloat16 or wider, within the bound.
A program may use at most 128 MiB of HBM per device.

v0:
```python
import functools

import jax
import jax.numpy as jnp
from jax import lax
from jax.experimental import pallas as pl
from jax.experimental.pallas import tpu as pltpu
from jax.sharding import PartitionSpec as P

HD = 64
WH = 6
WW = 12
SH = 3
SW = 6


def shifted_2(block, axis, distance):
    devices = range(lax.axis_size(axis))
    route = [((i - distance) % len(devices), i) for i in devices]
    return lax.ppermute(block, axis, route)


def layer_norm(values):
    average = jnp.mean(values, axis=-1, keepdims=True)
    centred = values - average
    spread = jnp.mean(centred * centred, axis=-1, keepdims=True)
    return centred * lax.rsqrt(spread + 1e-05)


def project(operand, matrix):
    flattened = operand.reshape(-1, operand.shape[-1])
    result = jnp.dot(flattened, matrix, preferred_element_type=jnp.float32)
    return result.reshape(operand.shape[:-1] + (matrix.shape[1],))


def project_back(operand, matrix):
    flattened = operand.reshape(-1, operand.shape[-1])
    result = lax.dot_general(
        flattened, matrix, (((1,), (1,)), ((), ())), preferred_element_type=jnp.float32
    )
    return result.reshape(operand.shape[:-1] + (matrix.shape[0],))


def window_attend(packed, labels, head_count):
    row_count, col_count = (packed.shape[0], packed.shape[1])
    row_wins, col_wins = (row_count // WH, col_count // WW)
    grouped = packed.reshape(row_wins, WH, col_wins, WW, head_count, 3, HD)
    grouped = grouped.transpose(0, 2, 4, 5, 1, 3, 6).reshape(
        row_wins, col_wins, head_count, 3, WH * WW, HD
    )
    queries = grouped[:, :, :, 0]
    key_rows = grouped[:, :, :, 1]
    value_rows = grouped[:, :, :, 2]
    scores = jnp.einsum(
        "abhqd,abhkd->abhqk", queries, key_rows, preferred_element_type=jnp.float32
    ) * HD ** (-0.5)
    if labels is not None:
        token_labels = jnp.broadcast_to(
            labels.reshape(row_wins, WH, 1), (row_wins, WH, WW)
        ).reshape(row_wins, 1, 1, WH * WW)
        same_region = token_labels[..., :, None] == token_labels[..., None, :]
        scores = jnp.where(same_region, scores, -jnp.inf)
    row_max = jnp.max(scores, axis=-1, keepdims=True)
    weights = jnp.exp(scores - row_max)
    normed_probs = (weights / jnp.sum(weights, axis=-1, keepdims=True)).astype(jnp.bfloat16)
    mixture = jnp.einsum(
        "abhqk,abhkd->abhqd", normed_probs, value_rows, preferred_element_type=jnp.float32
    ).astype(jnp.bfloat16)
    mixture = mixture.reshape(row_wins, col_wins, head_count, WH, WW, HD).transpose(
        0, 3, 1, 4, 2, 5
    )
    return mixture.reshape(row_count, col_count, head_count * HD)


def head_terms(normed, qkv_cols, out_cols):
    head_count = qkv_cols.shape[1] // (3 * HD)
    packed = project(normed, qkv_cols).astype(jnp.bfloat16)
    return project_back(window_attend(packed, None, head_count), out_cols)


def unit_terms(normed, up_cols, down_cols):
    hidden = jax.nn.gelu(project(normed, up_cols), approximate=False).astype(jnp.bfloat16)
    return project_back(hidden, down_cols)


BLK = 128
NT = (((1,), (1,)), ((), ()))


def softmax_mix(q, k, v, bias):
    scores = lax.dot_general(q, k, NT, preferred_element_type=jnp.float32) * HD ** (-0.5)
    if bias is not None:
        scores = scores + bias
    weights = jnp.exp(scores - jnp.max(scores, axis=-1, keepdims=True))
    probs = weights / jnp.sum(weights, axis=-1, keepdims=True)
    return jnp.dot(probs.astype(jnp.bfloat16), v, preferred_element_type=jnp.float32)


def fine_kernel(heads, qkv_ref, bias_ref, out_ref):
    bias = bias_ref[0]
    for pair in range(heads // 2):
        block = qkv_ref[0, :, pair * 6 * HD : (pair + 1) * 6 * HD]
        parts = [block[:, i * HD : (i + 1) * HD] for i in range(6)]
        mixed = [softmax_mix(*parts[3 * i : 3 * i + 3], bias) for i in range(2)]
        out_ref[0, :, pair * 2 * HD : (pair + 1) * 2 * HD] = jnp.concatenate(
            mixed, axis=1
        ).astype(jnp.bfloat16)


def fine_attend(qkv, bias):
    wins, size, width = qkv.shape
    per_row = wins // bias.shape[0]
    return pl.pallas_call(
        functools.partial(fine_kernel, width // (3 * HD)),
        out_shape=jax.ShapeDtypeStruct((wins, size, width // 3), jnp.bfloat16),
        grid=(wins,),
        in_specs=[
            pl.BlockSpec((1, size, width), lambda w: (w, 0, 0)),
            pl.BlockSpec((1, size, size), lambda w: (w // per_row, 0, 0)),
        ],
        out_specs=pl.BlockSpec((1, size, width // 3), lambda w: (w, 0, 0)),
        compiler_params=pltpu.CompilerParams(vmem_limit_bytes=32 * 2**20),
        cost_estimate=pl.CostEstimate(
            flops=4 * wins * size * size * width // 3,
            bytes_accessed=wins * size * width * 3,
            transcendentals=wins * size * size * width // (3 * HD),
        ),
    )(qkv, bias)


def coarse_attend_kernel(x_ref, qkv_ref, rows_ref, a0_ref, a1_ref, b0_ref, b1_ref, own_ref, peer_ref, sum_ref):
    lat = lax.axis_index("lat")
    count, width = x_ref.shape
    size, deep = WH * WW, width // 4
    shifts = a0_ref.shape[0] // 2
    halves_a, halves_b = (a0_ref, a1_ref), (b0_ref, b1_ref)

    def mixed_heads(qkv):
        rows = []
        for w in range(count // size):
            block = qkv[w * size : (w + 1) * size].astype(jnp.bfloat16)
            parts = [block[:, i * HD : (i + 1) * HD] for i in range(6)]
            rows.append(
                jnp.concatenate(
                    [softmax_mix(*parts[3 * i : 3 * i + 3], None) for i in range(2)], axis=1
                )
            )
        return jnp.concatenate(rows, axis=0).astype(jnp.bfloat16)

    def columns(j):
        return pl.ds(pl.multiple_of((lat ^ j) * deep, deep), deep)

    mixed = mixed_heads(jnp.dot(x_ref[...], qkv_ref[...], preferred_element_type=jnp.float32))
    sum_ref[...] = lax.dot_general(mixed, rows_ref[...], NT, preferred_element_type=jnp.float32)
    for s in range(shifts):
        qkv = None
        for j in range(4):
            first = halves_a[j // 2][(j % 2) * shifts + s]
            second = halves_b[j % 2][(j // 2) * shifts + s]
            block = jnp.concatenate([first[:deep], first[deep:], second[:deep]], axis=1)
            term = jnp.dot(x_ref[:, columns(j)], block, preferred_element_type=jnp.float32)
            qkv = term if qkv is None else qkv + term
        mixed = mixed_heads(qkv)
        for j in range(4):
            out_rows = halves_b[j % 2][(j // 2) * shifts + s][deep:]
            sum_ref[:, columns(j)] += lax.dot_general(
                mixed, out_rows, NT, preferred_element_type=jnp.float32
            )
    own_ref[...] = sum_ref[: count // 2]
    peer_ref[...] = sum_ref[count // 2 :].astype(jnp.bfloat16)


def coarse_attend(x, qkv, out, moved):
    count, width = x.shape
    whole = pl.BlockSpec(memory_space=pltpu.VMEM)
    return pl.pallas_call(
        coarse_attend_kernel,
        out_shape=(
            jax.ShapeDtypeStruct((count // 2, width), jnp.float32),
            jax.ShapeDtypeStruct((count // 2, width), jnp.bfloat16),
        ),
        in_specs=[whole] * 7,
        out_specs=(whole, whole),
        scratch_shapes=[pltpu.VMEM((count, width), jnp.float32)],
        compiler_params=pltpu.CompilerParams(vmem_limit_bytes=40 * 2**20),
        cost_estimate=pl.CostEstimate(
            flops=4 * count * width * width,
            bytes_accessed=4 * width * width,
            transcendentals=count * WH * WW * 8,
        ),
    )(x, qkv, out, *moved)


def coarse_mlp_kernel(x_ref, base_ref, *refs):
    ups, downs, out_ref = refs[: len(refs) // 2], refs[len(refs) // 2 : -1], refs[-1]

    @pl.when(pl.program_id(0) == 0)
    def _():
        out_ref[...] = base_ref[...]

    def joined(parts):
        parts = [part[...].reshape(part.shape[-2:]) for part in parts]
        return parts[0] if len(parts) == 1 else jnp.concatenate(parts, axis=1)

    wide = jnp.dot(x_ref[...], joined(ups), preferred_element_type=jnp.float32)
    hidden = (0.5 * wide * (1.0 + lax.erf(wide * 0.5**0.5))).astype(jnp.bfloat16)
    out_ref[...] += lax.dot_general(hidden, joined(downs), NT, preferred_element_type=jnp.float32)


def coarse_mlp(x, base, steps, operands, specs):
    count, width = x.shape
    whole = pl.BlockSpec((count, width), lambda s: (0, 0))
    hidden = steps * 4 * BLK
    return pl.pallas_call(
        coarse_mlp_kernel,
        out_shape=jax.ShapeDtypeStruct((count, width), jnp.float32),
        grid=(steps,),
        in_specs=[whole, whole] + specs,
        out_specs=whole,
        compiler_params=pltpu.CompilerParams(vmem_limit_bytes=40 * 2**20),
        cost_estimate=pl.CostEstimate(
            flops=4 * count * width * hidden,
            bytes_accessed=4 * width * hidden,
            transcendentals=count * hidden,
        ),
    )(x, base, *operands)


def own_mlp(x, up, down):
    base = jnp.zeros(x.shape, jnp.float32)
    return coarse_mlp(x, base, 1, [up, down], [pl.BlockSpec(up.shape, lambda s: (0, 0))] * 2)


def moved_mlp(x, base, moved):
    a0, a1, b0, b1 = moved
    shifts = a0.shape[0] // 2
    low = pl.BlockSpec((1,) + a0.shape[1:], lambda s: (s, 0, 0))
    high = pl.BlockSpec((1,) + a0.shape[1:], lambda s: (shifts + s, 0, 0))
    operands = [a0, a0, a1, a1, b0, b1, b0, b1]
    return coarse_mlp(x, base, shifts, operands, [low, high, low, high, low, low, high, high])


def swapped(block, axis, bit):
    return lax.ppermute(block, axis, [(i, i ^ bit) for i in range(lax.axis_size(axis))])


def along_lon(a, b):
    lons = lax.axis_size("lon")
    both = jnp.stack([a, b])
    return [
        lax.ppermute(both, "lon", [(i, (i + shift) % lons) for i in range(lons)])
        for shift in range(2, lons, 2)
    ]


def first_swap(got):
    a = jnp.stack([one[0] for one in got])
    b = jnp.stack([one[1] for one in got])
    return (a, swapped(a, "lat", 1), b, swapped(b, "lat", 2))


def second_swap(a, ax, b, by):
    a0, b0 = jnp.concatenate([a, ax], axis=0), jnp.concatenate([b, by], axis=0)
    return (a0, swapped(a0, "lat", 2), b0, swapped(b0, "lat", 1))


def level_parts(qkv, out, up, down):
    lat = lax.axis_index("lat")
    deep = qkv.shape[0] // 4
    qkv = lax.dynamic_slice_in_dim(qkv, lat * deep, deep, 0)
    out = lax.dynamic_slice_in_dim(out, lat * deep, deep, 0)
    first = jnp.concatenate([qkv[:, :BLK], qkv[:, BLK : 2 * BLK]], axis=0)
    second = jnp.concatenate([qkv[:, 2 * BLK :], out], axis=0)
    up = lax.dynamic_slice_in_dim(up, lat * BLK, BLK, 1)
    return (first, second), (up, lax.dynamic_slice_in_dim(down, lat * BLK, BLK, 1))


def local_level(tokens, attend_moved, mlp_moved, qkv, out, up, down):
    count = tokens.shape[0]

    def shared(values):
        normed = layer_norm(values).astype(jnp.bfloat16)
        return jnp.concatenate([normed, swapped(normed, "lon", 1)], axis=0)

    own, peer = coarse_attend(shared(tokens), qkv, out, attend_moved)
    tokens = tokens + own + swapped(peer, "lon", 1).astype(jnp.float32)
    both = shared(tokens)
    total = own_mlp(both, up, down)
    for moved in mlp_moved:
        total = moved_mlp(both, total, moved)
    peer = swapped(total[count:].astype(jnp.bfloat16), "lon", 1)
    return (tokens + total[:count] + peer.astype(jnp.float32)).astype(jnp.bfloat16)


def per_device(
    tokens,
    fine_qkv,
    fine_out,
    fine_up,
    fine_down,
    merge_weight,
    coarse_qkv,
    coarse_out,
    coarse_up,
    coarse_down,
    split_weight,
):
    band_rows, band_cols = (tokens.shape[0], tokens.shape[1])
    total_rows = band_rows * lax.axis_size("lat")
    lat_index = lax.axis_index("lat")
    whole_weights = (
        lax.axis_size("lat") == 4 and coarse_up.shape[1] == 4 * BLK and coarse_qkv.shape[1] == 3 * BLK
    )
    if whole_weights:
        attend_part, mlp_part = level_parts(coarse_qkv, coarse_out, coarse_up, coarse_down)
        attend_moved, mlp_moved = (along_lon(*attend_part), along_lon(*mlp_part))
    stream = tokens.astype(jnp.float32)
    normed = layer_norm(stream).astype(jnp.bfloat16)
    below_rows = shifted_2(normed[:SH], "lat", -1)
    shifted = jnp.concatenate([normed[SH:], below_rows], axis=0)
    east_cols = shifted_2(shifted[:, :SW], "lon", -1)
    shifted = jnp.concatenate([shifted[:, SW:], east_cols], axis=1)
    anchor = (lat_index * band_rows + jnp.arange(band_rows, dtype=jnp.int32) + SH) % total_rows
    labels = (anchor < SH).astype(jnp.int32)
    row_wins, col_wins = (band_rows // WH, band_cols // WW)
    window_labels = jnp.repeat(labels.reshape(row_wins, WH), WW, axis=1)
    same_region = window_labels[:, :, None] == window_labels[:, None, :]
    bias = jnp.where(same_region, 0.0, -jnp.inf).astype(jnp.float32)
    shifted = (
        shifted.reshape(row_wins, WH, col_wins, WW, -1)
        .transpose(0, 2, 1, 3, 4)
        .reshape(row_wins * col_wins, WH * WW, -1)
    )
    packed = project(shifted, fine_qkv).astype(jnp.bfloat16)
    if whole_weights:
        packed, attend_moved = lax.optimization_barrier((packed, attend_moved))
        attend_moved = first_swap(attend_moved)
    attended = fine_attend(packed, bias)
    if whole_weights:
        near, middle, far = mlp_moved
        attended, attend_moved, near = lax.optimization_barrier((attended, attend_moved, near))
        attend_moved = second_swap(*attend_moved)
        near = first_swap([near])
    attended = (
        attended.reshape(row_wins, col_wins, WH, WW, -1)
        .transpose(0, 2, 1, 3, 4)
        .reshape(band_rows, band_cols, -1)
    )
    above_rows = shifted_2(attended[band_rows - SH :], "lat", 1)
    attended = jnp.concatenate([above_rows, attended[: band_rows - SH]], axis=0)
    west_cols = shifted_2(attended[:, band_cols - SW :], "lon", 1)
    attended = jnp.concatenate([west_cols, attended[:, : band_cols - SW]], axis=1)
    if whole_weights:
        attended, near, far = lax.optimization_barrier((attended, near, far))
        far = first_swap([far])
        near = second_swap(*near)
    stream = stream + project(attended, fine_out)
    hidden = jax.nn.gelu(
        project(layer_norm(stream).astype(jnp.bfloat16), fine_up), approximate=False
    ).astype(jnp.bfloat16)
    if whole_weights:
        hidden, far, middle = lax.optimization_barrier((hidden, far, middle))
        middle = first_swap([middle])
        far = second_swap(*far)
    skip_tokens = (stream + project(hidden, fine_down)).astype(jnp.bfloat16)
    skip_tokens = lax.optimization_barrier(skip_tokens)
    coarse_rows, coarse_cols = (band_rows // 2, band_cols // 2)
    wins = (coarse_rows // WH, WH, 2, coarse_cols // WW, WW, 2)
    merged = (
        skip_tokens.reshape(wins + (-1,))
        .transpose(0, 3, 1, 4, 2, 5, 6)
        .reshape(coarse_rows * coarse_cols, -1)
    )
    merged = lax.optimization_barrier(merged)
    coarse = project(
        layer_norm(merged.astype(jnp.float32)).astype(jnp.bfloat16), merge_weight
    ).astype(jnp.bfloat16)
    coarse_float = coarse.astype(jnp.float32)
    if whole_weights:
        coarse_float, middle = lax.optimization_barrier((coarse_float, middle))
        mlp_moved = (near, far, second_swap(*middle))
        level_state = local_level(
            coarse_float, attend_moved, mlp_moved, coarse_qkv, coarse_out, coarse_up, coarse_down
        )
    else:
        coarse_float = (
            coarse_float.reshape(wins[0], wins[3], WH, WW, -1)
            .transpose(0, 2, 1, 3, 4)
            .reshape(coarse_rows, coarse_cols, -1)
        )
        gathered = lax.all_gather(
            layer_norm(coarse_float).astype(jnp.bfloat16), "lon", axis=1, tiled=True
        )
        level_state = coarse_float + lax.psum_scatter(
            head_terms(gathered, coarse_qkv, coarse_out).astype(jnp.bfloat16),
            "lon",
            scatter_dimension=1,
            tiled=True,
        ).astype(jnp.float32)
        unit_total = unit_terms(
            lax.all_gather(layer_norm(level_state).astype(jnp.bfloat16), "lon", axis=1, tiled=True),
            coarse_up,
            coarse_down,
        )
        level_state = (
            level_state
            + lax.psum_scatter(
                unit_total.astype(jnp.bfloat16), "lon", scatter_dimension=1, tiled=True
            ).astype(jnp.float32)
        ).astype(jnp.bfloat16)
        level_state = (
            level_state.reshape(wins[0], WH, wins[3], WW, -1)
            .transpose(0, 2, 1, 3, 4)
            .reshape(coarse_rows * coarse_cols, -1)
        )
    expanded = project(level_state, split_weight)
    expanded = (
        expanded.reshape(wins[0], wins[3], WH, WW, 2, 2, -1)
        .transpose(0, 2, 4, 1, 3, 5, 6)
        .reshape(band_rows, band_cols, -1)
    )
    return (skip_tokens.astype(jnp.float32) + layer_norm(expanded)).astype(jnp.bfloat16)


def solution(mesh):
    return jax.shard_map(
        per_device,
        mesh=mesh,
        in_specs=(
            P("lat", "lon", None),
            P(),
            P(),
            P(),
            P(),
            P(),
            P(None, "lon"),
            P(None, "lon"),
            P(None, "lon"),
            P(None, "lon"),
            P(),
        ),
        out_specs=P("lat", "lon", None),
        check_vma=False,
    )
```

profile of v0, /device:TPU:21, one launch (start us, length us, event | category | flops | bytes accessed | tf_op | source)
XLA Modules:
  0.0 181.9 jit_solution(17395716416250439178)
XLA Ops:
  12.8 2.3 %collective-permute-start.1 = (bf16[12,6,512]{2,1,0:T(8,128)(2,1)S(1)}, bf16[12,6,512]{2,1,0:T(8,128)(2,1)S(1)}, u32[]{:S(2)}, u32[]{:S(2)}) collective-permute-start(bf16[12,6,512]{2,1,0:T(8,128)(2,1)S(1)} %pad_maximum_fusion.9), channel_id=1, source_target_pairs={{1,0},{2,1},{3,2},{4,3},{5,4},{6,5},{7,6},{0,7},{9,8},{10,9},{11,1... | collective-permute-start | bytes 221192 | tf_op jit(solution)/shard_map/ppermute | solution.py:20
  15.2 18.8 %collective-permute-done.1 = bf16[12,6,512]{2,1,0:T(8,128)(2,1)S(1)} collective-permute-done((bf16[12,6,512]{2,1,0:T(8,128)(2,1)S(1)}, bf16[12,6,512]{2,1,0:T(8,128)(2,1)S(1)}, u32[]{:S(2)}, u32[]{:S(2)}) %collective-permute-start.1) | collective-permute-done | bytes 73760 | tf_op jit(solution)/shard_map/ppermute | solution.py:20
  36.5 3.7 %convolution_convert_fusion.qkv_ref = bf16[8,72,1536]{2,1,0:T(8,128)(2,1)} fusion(bf16[8,72,512]{2,1,0:T(8,128)(2,1)S(1)} %reshape.140, bf16[512,1536]{1,0:T(8,128)(2,1)} %param.12), kind=kOutput, calls=%fused_computation.19 | convolution fusion | flops 906854400 | bytes 3932160 | tf_op jit(solution)/shard_map/dot_general | solution.py:32
  44.9 6.4 %collective-permute-start.12 = (bf16[2,1024,128]{2,1,0:T(8,128)(2,1)}, bf16[2,1024,128]{2,1,0:T(8,128)(2,1)}, u32[]{:S(2)}, u32[]{:S(2)}) collective-permute-start(bf16[2,1024,128]{2,1,0:T(8,128)(2,1)} %pad_maximum_fusion.4), channel_id=1, source_target_pairs={{0,6},{1,7},{2,0},{3,1},{4,2},{5,3},{6,4},{7,5},{8,14},{9,15},{10,... | collective-permute-start | bytes 1572872 | tf_op jit(solution)/shard_map/ppermute | solution.py:251
  53.0 8.4 %shard_map.109 = bf16[8,72,512]{2,1,0:T(8,128)(2,1)S(1)} custom-call(bf16[8,72,1536]{2,1,0:T(8,128)(2,1)S(1)} %copy-done.2, f32[2,72,72]{2,1,0:T(8,128)S(1)} %compare_select_fusion.bias_ref), custom_call_target="tpu_custom_call" | custom-call | flops 84934656 | bytes 2654208 | tf_op jit(solution)/shard_map/pallas_call | solution.py:113
  64.4 2.1 %collective-permute-start.10 = (bf16[1,1024,128]{2,1,0:T(8,128)(2,1)S(1)}, bf16[1,1024,128]{2,1,0:T(8,128)(2,1)S(1)}, u32[]{:S(2)}, u32[]{:S(2)}) collective-permute-start(bf16[1,1024,128]{2,1,0:T(8,128)(2,1)S(1)} %get-tuple-element.51), channel_id=1, source_target_pairs={{0,8},{8,0},{16,24},{24,16},{1,9},{9,1},{17,25},{25,17},{2,10},{10... | collective-permute-start | bytes 786440 | tf_op jit(solution)/shard_map/ppermute | solution.py:244
  66.8 1.8 constant_dynamic-update-slice_fusion.1
  69.6 1.8 constant_dynamic-update-slice_fusion.a0_ref
  71.4 1.8 collective-permute-start.9
  73.2 9.5 %collective-permute-done.9 = bf16[12,6,512]{2,1,0:T(8,128)(2,1)S(1)} collective-permute-done((bf16[12,6,512]{2,1,0:T(8,128)(2,1)S(1)}, bf16[12,6,512]{2,1,0:T(8,128)(2,1)S(1)}, u32[]{:S(2)}, u32[]{:S(2)}) %collective-permute-start.9) | collective-permute-done | bytes 73760 | tf_op jit(solution)/shard_map/ppermute | solution.py:20
  88.0 12.3 %fusion.2 = bf16[12,48,2048]{2,1,0:T(8,128)(2,1)S(1)} fusion(bf16[512,2048]{1,0:T(8,128)(2,1)S(1)} %copy-done, f32[12,48,512]{2,1,0:T(8,128)S(1)} %get-tuple-element.81, f32[12,48]{1,0:T(8,128)S(1)} %add_rsqrt_fusion.1, f32[12,48]{1,0:T(8,128)S(1)} %broadcast_multiply_fusion.1), kind=kOutput, calls=%fused_computation.3 | convolution fusion | flops 1285521408 | bytes 5640704 | tf_op jit(solution)/shard_map/dot_general | solution.py:32
  101.7 5.5 %collective-permute-done.13 = bf16[1,1024,128]{2,1,0:T(8,128)(2,1)S(1)} collective-permute-done((bf16[1,1024,128]{2,1,0:T(8,128)(2,1)S(1)}, bf16[1,1024,128]{2,1,0:T(8,128)(2,1)S(1)}, u32[]{:S(2)}, u32[]{:S(2)}) %collective-permute-start.13) | collective-permute-done | bytes 262176 | tf_op jit(solution)/shard_map/ppermute | solution.py:244
  107.9 2.2 %fusion.24 = bf16[12,48,512]{2,1,0:T(8,128)(2,1)} fusion(f32[12,48,512]{2,1,0:T(8,128)S(1)} %get-tuple-element.81, bf16[12,48,2048]{2,1,0:T(8,128)(2,1)S(1)} %fusion.2, bf16[2048,512]{1,0:T(8,128)(2,1)S(1)} %copy-done.26), kind=kOutput, calls=%fused_computation.35 | convolution fusion | flops 1208549376 | bytes 6225920 | tf_op jit(solution)/shard_map/dot_general | solution.py:32
  110.1 1.9 %reshape.132 = bf16[1,6,2,2,12,2,512]{6,5,4,3,2,1,0:T(2,128)(2,1)S(1)} reshape(bf16[12,48,512]{2,1,0:T(8,128)(2,1)} %fusion.24) | data formatting | bytes 1179648 | tf_op jit(solution)/shard_map/reshape | solution.py:370
  113.4 2.4 %reshape.133 = bf16[144,2048]{1,0:T(8,128)(2,1)S(1)} reshape(bf16[1,2,6,12,2,2,512]{6,5,4,3,2,1,0:T(2,128)(2,1)} %bitcast.49) | data formatting | bytes 1179648 | tf_op jit(solution)/shard_map/reshape | solution.py:372
  118.1 3.2 %fusion.27 = f32[144,1024]{1,0:T(8,128)S(1)} fusion(bf16[2048,1024]{1,0:T(8,128)(2,1)} %param.16, bf16[144,2048]{1,0:T(8,128)(2,1)} %copy-done.7, f32[144]{0:T(256)S(1)} %add_rsqrt_fusion.5, f32[144]{0:T(256)S(1)} %broadcast_multiply_fusion.5), kind=kOutput, calls=%fused_computation.37 | convolution fusion | flops 605454336 | bytes 5375104 | tf_op jit(solution)/shard_map/dot_general | solution.py:32
  123.9 3.9 %collective-permute-start.18 = (bf16[144,1024]{1,0:T(8,128)(2,1)S(1)}, bf16[144,1024]{1,0:T(8,128)(2,1)S(1)}, u32[]{:S(2)}, u32[]{:S(2)}) collective-permute-start(bf16[144,1024]{1,0:T(8,128)(2,1)S(1)} %multiply_convert_fusion.3), channel_id=1, source_target_pairs={{0,1},{1,0},{2,3},{3,2},{4,5},{5,4},{6,7},{7,6},{8,9},{9,8},{10,11... | collective-permute-start | bytes 884744 | tf_op jit(solution)/shard_map/ppermute | solution.py:244
  134.5 7.0 %shard_map.110 = (f32[144,1024]{1,0:T(8,128)S(1)}, bf16[144,1024]{1,0:T(8,128)(2,1)S(1)}) custom-call(bf16[288,1024]{1,0:T(8,128)(2,1)S(1)} %pad_maximum_fusion.2.x_ref, bf16[1024,384]{1,0:T(8,128)(2,1)S(1)} %copy-done.5, bf16[1024,128]{1,0:T(8,128)(2,1)S(1)} %copy-done.6, bf16[6,512,128]{2,1,0:T(8,128)(2,1)} %constant_dynamic-update-slice_fusion.a0_ref, ...), custom_call_target="tpu_custom_call" | custom-call | flops 1207959552 | bytes 4194304 | tf_op jit(solution)/shard_map/pallas_call | solution.py:176
  149.0 7.6 %collective-permute-done.26.refs_5_.refs_7_ = bf16[2,1024,128]{2,1,0:T(8,128)(2,1)S(1)} collective-permute-done((bf16[2,1024,128]{2,1,0:T(8,128)(2,1)S(1)}, bf16[2,1024,128]{2,1,0:T(8,128)(2,1)S(1)}, u32[]{:S(2)}, u32[]{:S(2)}) %collective-permute-start.26) | collective-permute-done | bytes 524320 | tf_op jit(solution)/shard_map/ppermute | solution.py:244
  159.0 8.9 %collective-permute-done.28.refs_5_.refs_7_ = bf16[2,1024,128]{2,1,0:T(8,128)(2,1)S(1)} collective-permute-done((bf16[2,1024,128]{2,1,0:T(8,128)(2,1)S(1)}, bf16[2,1024,128]{2,1,0:T(8,128)(2,1)S(1)}, u32[]{:S(2)}, u32[]{:S(2)}) %collective-permute-start.28) | collective-permute-done | bytes 524320 | tf_op jit(solution)/shard_map/ppermute | solution.py:244
  172.8 1.6 copy.29
  174.8 1.6 multiply_reduce_fusion
  176.5 2.1 %reshape.135 = f32[12,48,512]{2,1,0:T(8,128)S(1)} reshape(f32[1,6,2,2,12,2,512]{6,5,4,3,2,1,0:T(2,128)} %bitcast.47) | data formatting | bytes 2359296 | tf_op jit(solution)/shard_map/reshape | solution.py:420
  179.7 2.2 %add_convert_fusion = bf16[12,48,512]{2,1,0:T(8,128)(2,1)} fusion(f32[12,48,512]{2,1,0:T(8,128)S(1)} %reshape.135, bf16[12,48,512]{2,1,0:T(8,128)(2,1)} %fusion.24, f32[12,48]{1,0:T(8,128)S(1)} %rsqrt.57, f32[12,48]{1,0:T(8,128)S(1)} %div.49), kind=kLoop, calls=%fused_computation.43 | loop fusion | flops 1474560 | bytes 2363904 | tf_op jit(solution)/shard_map/convert_element_type | solution.py:422
  (191 shorter events, 62.2 us)
Async XLA Ops:
  1.9 38.3 %collective-permute-start.2 = (bf16[2,512,128]{2,1,0:T(8,128)(2,1)}, bf16[2,512,128]{2,1,0:T(8,128)(2,1)}, u32[]{:S(2)}, u32[]{:S(2)}) collective-permute-start(bf16[2,512,128]{2,1,0:T(8,128)(2,1)} %pad_maximum_fusion.7), channel_id=1, source_target_pairs={{0,2},{1,3},{2,4},{3,5},{4,6},{5,7},{6,0},{7,1},{8,10},{9,11},{10,... | collective-permute-start | bytes 786440 | tf_op jit(solution)/shard_map/ppermute | solution.py:251
  3.2 37.0 %collective-permute-start.3 = (bf16[2,512,128]{2,1,0:T(8,128)(2,1)}, bf16[2,512,128]{2,1,0:T(8,128)(2,1)}, u32[]{:S(2)}, u32[]{:S(2)}) collective-permute-start(bf16[2,512,128]{2,1,0:T(8,128)(2,1)} %pad_maximum_fusion.7), channel_id=1, source_target_pairs={{0,4},{1,5},{2,6},{3,7},{4,0},{5,1},{6,2},{7,3},{8,12},{9,13},{10,... | collective-permute-start | bytes 786440 | tf_op jit(solution)/shard_map/ppermute | solution.py:251
  3.3 37.0 %collective-permute-start.4 = (bf16[2,512,128]{2,1,0:T(8,128)(2,1)}, bf16[2,512,128]{2,1,0:T(8,128)(2,1)}, u32[]{:S(2)}, u32[]{:S(2)}) collective-permute-start(bf16[2,512,128]{2,1,0:T(8,128)(2,1)} %pad_maximum_fusion.7), channel_id=1, source_target_pairs={{0,6},{1,7},{2,0},{3,1},{4,2},{5,3},{6,4},{7,5},{8,14},{9,15},{10,... | collective-permute-start | bytes 786440 | tf_op jit(solution)/shard_map/ppermute | solution.py:251
  11.5 50.0 %collective-permute-start.7 = (bf16[2,1024,128]{2,1,0:T(8,128)(2,1)}, bf16[2,1024,128]{2,1,0:T(8,128)(2,1)}, u32[]{:S(2)}, u32[]{:S(2)}) collective-permute-start(bf16[2,1024,128]{2,1,0:T(8,128)(2,1)} %pad_maximum_fusion.4), channel_id=1, source_target_pairs={{0,2},{1,3},{2,4},{3,5},{4,6},{5,7},{6,0},{7,1},{8,10},{9,11},{10,... | collective-permute-start | bytes 1572872 | tf_op jit(solution)/shard_map/ppermute | solution.py:251
  12.8 21.3 %collective-permute-start.1 = (bf16[12,6,512]{2,1,0:T(8,128)(2,1)S(1)}, bf16[12,6,512]{2,1,0:T(8,128)(2,1)S(1)}, u32[]{:S(2)}, u32[]{:S(2)}) collective-permute-start(bf16[12,6,512]{2,1,0:T(8,128)(2,1)S(1)} %pad_maximum_fusion.9), channel_id=1, source_target_pairs={{1,0},{2,1},{3,2},{4,3},{5,4},{6,5},{7,6},{0,7},{9,8},{10,9},{11,1... | collective-permute-start | bytes 221192 | tf_op jit(solution)/shard_map/ppermute | solution.py:20
  43.3 18.2 %collective-permute-start.5 = (bf16[3,512,128]{2,1,0:T(8,128)(2,1)S(1)}, bf16[3,512,128]{2,1,0:T(8,128)(2,1)}, u32[]{:S(2)}, u32[]{:S(2)}) collective-permute-start(bf16[3,512,128]{2,1,0:T(8,128)(2,1)S(1)} %pad_maximum_fusion.5), channel_id=1, source_target_pairs={{0,8},{8,0},{16,24},{24,16},{1,9},{9,1},{17,25},{25,17},{2,10},{10... | collective-permute-start | bytes 1179656 | tf_op jit(solution)/shard_map/ppermute | solution.py:244
  44.6 16.9 %collective-permute-start.6 = (bf16[3,512,128]{2,1,0:T(8,128)(2,1)S(1)}, bf16[3,512,128]{2,1,0:T(8,128)(2,1)S(1)}, u32[]{:S(2)}, u32[]{:S(2)}) collective-permute-start(bf16[3,512,128]{2,1,0:T(8,128)(2,1)S(1)} %pad_maximum_fusion.6), channel_id=1, source_target_pairs={{0,16},{8,24},{16,0},{24,8},{1,17},{9,25},{17,1},{25,9},{2,18},{10... | collective-permute-start | bytes 1179656 | tf_op jit(solution)/shard_map/ppermute | solution.py:244
  44.9 39.3 %collective-permute-start.12 = (bf16[2,1024,128]{2,1,0:T(8,128)(2,1)}, bf16[2,1024,128]{2,1,0:T(8,128)(2,1)}, u32[]{:S(2)}, u32[]{:S(2)}) collective-permute-start(bf16[2,1024,128]{2,1,0:T(8,128)(2,1)} %pad_maximum_fusion.4), channel_id=1, source_target_pairs={{0,6},{1,7},{2,0},{3,1},{4,2},{5,3},{6,4},{7,5},{8,14},{9,15},{10,... | collective-permute-start | bytes 1572872 | tf_op jit(solution)/shard_map/ppermute | solution.py:251
  51.2 49.2 %collective-permute-start.15 = (bf16[2,1024,128]{2,1,0:T(8,128)(2,1)}, bf16[2,1024,128]{2,1,0:T(8,128)(2,1)}, u32[]{:S(2)}, u32[]{:S(2)}) collective-permute-start(bf16[2,1024,128]{2,1,0:T(8,128)(2,1)} %pad_maximum_fusion.4), channel_id=1, source_target_pairs={{0,4},{1,5},{2,6},{3,7},{4,0},{5,1},{6,2},{7,3},{8,12},{9,13},{10,... | collective-permute-start | bytes 1572872 | tf_op jit(solution)/shard_map/ppermute | solution.py:251
  63.0 8.5 %collective-permute-start.8 = (bf16[3,48,512]{2,1,0:T(8,128)(2,1)S(1)}, bf16[3,48,512]{2,1,0:T(8,128)(2,1)S(1)}, u32[]{:S(2)}, u32[]{:S(2)}) collective-permute-start(bf16[3,48,512]{2,1,0:T(8,128)(2,1)S(1)} %slice.105), channel_id=1, source_target_pairs={{24,0},{0,8},{8,16},{16,24},{25,1},{1,9},{9,17},{17,25},{26,2},{2,... | collective-permute-start | bytes 442376 | tf_op jit(solution)/shard_map/ppermute | solution.py:20
  64.4 20.1 %collective-permute-start.10 = (bf16[1,1024,128]{2,1,0:T(8,128)(2,1)S(1)}, bf16[1,1024,128]{2,1,0:T(8,128)(2,1)S(1)}, u32[]{:S(2)}, u32[]{:S(2)}) collective-permute-start(bf16[1,1024,128]{2,1,0:T(8,128)(2,1)S(1)} %get-tuple-element.51), channel_id=1, source_target_pairs={{0,8},{8,0},{16,24},{24,16},{1,9},{9,1},{17,25},{25,17},{2,10},{10... | collective-permute-start | bytes 786440 | tf_op jit(solution)/shard_map/ppermute | solution.py:244
  66.6 17.9 %collective-permute-start.11 = (bf16[1,1024,128]{2,1,0:T(8,128)(2,1)S(1)}, bf16[1,1024,128]{2,1,0:T(8,128)(2,1)S(1)}, u32[]{:S(2)}, u32[]{:S(2)}) collective-permute-start(bf16[1,1024,128]{2,1,0:T(8,128)(2,1)S(1)} %get-tuple-element.53), channel_id=1, source_target_pairs={{0,16},{8,24},{16,0},{24,8},{1,17},{9,25},{17,1},{25,9},{2,18},{10... | collective-permute-start | bytes 786440 | tf_op jit(solution)/shard_map/ppermute | solution.py:244
  71.4 11.3 %collective-permute-start.9 = (bf16[12,6,512]{2,1,0:T(8,128)(2,1)S(1)}, bf16[12,6,512]{2,1,0:T(8,128)(2,1)S(1)}, u32[]{:S(2)}, u32[]{:S(2)}) collective-permute-start(bf16[12,6,512]{2,1,0:T(8,128)(2,1)S(1)} %pad_maximum_fusion.8), channel_id=1, source_target_pairs={{7,0},{0,1},{1,2},{2,3},{3,4},{4,5},{5,6},{6,7},{15,8},{8,9},{9,10... | collective-permute-start | bytes 221192 | tf_op jit(solution)/shard_map/ppermute | solution.py:20
  82.7 50.6 %collective-permute-start.19 = (bf16[6,512,128]{2,1,0:T(8,128)(2,1)}, bf16[6,512,128]{2,1,0:T(8,128)(2,1)}, u32[]{:S(2)}, u32[]{:S(2)}) collective-permute-start(bf16[6,512,128]{2,1,0:T(8,128)(2,1)} %constant_dynamic-update-slice_fusion.a0_ref), channel_id=1, source_target_pairs={{0,16},{8,24},{16,0},{24,8},{1,17},{9,25},{17,1},{25,9},{2,18},{10... | collective-permute-start | bytes 2359304 | tf_op jit(solution)/shard_map/ppermute | solution.py:244
  84.2 49.2 %collective-permute-start.20 = (bf16[6,512,128]{2,1,0:T(8,128)(2,1)S(1)}, bf16[6,512,128]{2,1,0:T(8,128)(2,1)}, u32[]{:S(2)}, u32[]{:S(2)}) collective-permute-start(bf16[6,512,128]{2,1,0:T(8,128)(2,1)S(1)} %constant_dynamic-update-slice_fusion.2.b0_ref), channel_id=1, source_target_pairs={{0,8},{8,0},{16,24},{24,16},{1,9},{9,1},{17,25},{25,17},{2,10},{10... | collective-permute-start | bytes 2359304 | tf_op jit(solution)/shard_map/ppermute | solution.py:244
  86.5 20.8 %collective-permute-start.13 = (bf16[1,1024,128]{2,1,0:T(8,128)(2,1)S(1)}, bf16[1,1024,128]{2,1,0:T(8,128)(2,1)S(1)}, u32[]{:S(2)}, u32[]{:S(2)}) collective-permute-start(bf16[1,1024,128]{2,1,0:T(8,128)(2,1)S(1)} %get-tuple-element.55), channel_id=1, source_target_pairs={{0,8},{8,0},{16,24},{24,16},{1,9},{9,1},{17,25},{25,17},{2,10},{10... | collective-permute-start | bytes 786440 | tf_op jit(solution)/shard_map/ppermute | solution.py:244
  87.8 20.2 %collective-permute-start.14 = (bf16[1,1024,128]{2,1,0:T(8,128)(2,1)S(1)}, bf16[1,1024,128]{2,1,0:T(8,128)(2,1)}, u32[]{:S(2)}, u32[]{:S(2)}) collective-permute-start(bf16[1,1024,128]{2,1,0:T(8,128)(2,1)S(1)} %get-tuple-element.57), channel_id=1, source_target_pairs={{0,16},{8,24},{16,0},{24,8},{1,17},{9,25},{17,1},{25,9},{2,18},{10... | collective-permute-start | bytes 786440 | tf_op jit(solution)/shard_map/ppermute | solution.py:244
  100.4 45.2 %collective-permute-start.23 = (bf16[2,1024,128]{2,1,0:T(8,128)(2,1)S(1)}, bf16[2,1024,128]{2,1,0:T(8,128)(2,1)S(1)}, u32[]{:S(2)}, u32[]{:S(2)}) collective-permute-start(bf16[2,1024,128]{2,1,0:T(8,128)(2,1)S(1)} %constant_dynamic-update-slice_fusion.4.refs_0_.refs_1_), channel_id=1, source_target_pairs={{0,16},{8,24},{16,0},{24,8},{1,17},{9,25},{17,1},{25,9},{2,18},{10... | collective-permute-start | bytes 1572872 | tf_op jit(solution)/shard_map/ppermute | solution.py:244
  123.9 8.0 %collective-permute-start.18 = (bf16[144,1024]{1,0:T(8,128)(2,1)S(1)}, bf16[144,1024]{1,0:T(8,128)(2,1)S(1)}, u32[]{:S(2)}, u32[]{:S(2)}) collective-permute-start(bf16[144,1024]{1,0:T(8,128)(2,1)S(1)} %multiply_convert_fusion.3), channel_id=1, source_target_pairs={{0,1},{1,0},{2,3},{3,2},{4,5},{5,4},{6,7},{7,6},{8,9},{9,8},{10,11... | collective-permute-start | bytes 884744 | tf_op jit(solution)/shard_map/ppermute | solution.py:244
  128.8 19.3 %collective-permute-start.24 = (bf16[2,1024,128]{2,1,0:T(8,128)(2,1)S(1)}, bf16[2,1024,128]{2,1,0:T(8,128)(2,1)S(1)}, u32[]{:S(2)}, u32[]{:S(2)}) collective-permute-start(bf16[2,1024,128]{2,1,0:T(8,128)(2,1)S(1)} %constant_dynamic-update-slice_fusion.6.refs_4_.refs_6_), channel_id=1, source_target_pairs={{0,8},{8,0},{16,24},{24,16},{1,9},{9,1},{17,25},{25,17},{2,10},{10... | collective-permute-start | bytes 1572872 | tf_op jit(solution)/shard_map/ppermute | solution.py:244
  132.0 17.1 %collective-permute-start.25 = (bf16[2,1024,128]{2,1,0:T(8,128)(2,1)S(1)}, bf16[2,1024,128]{2,1,0:T(8,128)(2,1)S(1)}, u32[]{:S(2)}, u32[]{:S(2)}) collective-permute-start(bf16[2,1024,128]{2,1,0:T(8,128)(2,1)S(1)} %constant_dynamic-update-slice_fusion.8.refs_0_.refs_1_), channel_id=1, source_target_pairs={{0,16},{8,24},{16,0},{24,8},{1,17},{9,25},{17,1},{25,9},{2,18},{10... | collective-permute-start | bytes 1572872 | tf_op jit(solution)/shard_map/ppermute | solution.py:244
  143.1 13.6 %collective-permute-start.26 = (bf16[2,1024,128]{2,1,0:T(8,128)(2,1)S(1)}, bf16[2,1024,128]{2,1,0:T(8,128)(2,1)S(1)}, u32[]{:S(2)}, u32[]{:S(2)}) collective-permute-start(bf16[2,1024,128]{2,1,0:T(8,128)(2,1)S(1)} %constant_dynamic-update-slice_fusion.10.refs_4_.refs_6_), channel_id=1, source_target_pairs={{0,8},{8,0},{16,24},{24,16},{1,9},{9,1},{17,25},{25,17},{2,10},{10... | collective-permute-start | bytes 1572872 | tf_op jit(solution)/shard_map/ppermute | solution.py:244
  145.6 13.4 %collective-permute-start.27 = (bf16[2,1024,128]{2,1,0:T(8,128)(2,1)S(1)}, bf16[2,1024,128]{2,1,0:T(8,128)(2,1)S(1)}, u32[]{:S(2)}, u32[]{:S(2)}) collective-permute-start(bf16[2,1024,128]{2,1,0:T(8,128)(2,1)S(1)} %constant_dynamic-update-slice_fusion.12.refs_0_.refs_1_), channel_id=1, source_target_pairs={{0,16},{8,24},{16,0},{24,8},{1,17},{9,25},{17,1},{25,9},{2,18},{10... | collective-permute-start | bytes 1572872 | tf_op jit(solution)/shard_map/ppermute | solution.py:244
  145.9 22.0 %collective-permute-start.28 = (bf16[2,1024,128]{2,1,0:T(8,128)(2,1)S(1)}, bf16[2,1024,128]{2,1,0:T(8,128)(2,1)S(1)}, u32[]{:S(2)}, u32[]{:S(2)}) collective-permute-start(bf16[2,1024,128]{2,1,0:T(8,128)(2,1)S(1)} %constant_dynamic-update-slice_fusion.14.refs_4_.refs_6_), channel_id=1, source_target_pairs={{0,8},{8,0},{16,24},{24,16},{1,9},{9,1},{17,25},{25,17},{2,10},{10... | collective-permute-start | bytes 1572872 | tf_op jit(solution)/shard_map/ppermute | solution.py:244
  (33 other events, 331.5 us)
where the time goes:
time: 183 us; the launch traced here: 182 us
  waiting for transfers between devices  55.4 us (30%)
  local copies, waits for them, and re-layouts  37.1 us (20%)
  starting transfers between devices  33.7 us (18%)
  matrix products  22.8 us (12%)
  Pallas kernels  19 us (10%)
  other arithmetic  13.1 us (7%)
    ppermute x4, waiting for transfers between devices, shifted_2(): return lax.ppermute(block, axis, route)  29.3 us
    ppermute x20, waiting for transfers between devices, swapped(): lax.ppermute(block, axis, [(i, i ^ bit) for i in range(lax.axis_size(axis...  26.1 us
    dot_general x6, matrix products, project(): result = jnp.dot(flattened, matrix, preferred_element_type=jnp.float32)  22.8 us
    ppermute x20, starting transfers between devices, swapped(): lax.ppermute(block, axis, [(i, i ^ bit) for i in range(lax.axis_size(axis...  19 us
    ppermute x6, starting transfers between devices, along_lon(): lax.ppermute(both, 'lon', [(i, (i + shift) % lons) for i in range(lons)])  9.18 us
    unnamed x62, local copies, waits for them, and re-layouts  8.85 us
    pallas_call x1, Pallas kernels, fine_attend(): pl.pallas_call(functools.partial(fine_kernel, width // (3 * HD)), out_sha...  8.43 us
    pallas_call x1, Pallas kernels, coarse_attend(): pl.pallas_call(coarse_attend_kernel, out_shape=(jax.ShapeDtypeStruct((cou...  6.96 us
  transfers between devices with their start and end apart: 30, of which 9 were waited for; matrix products, arithmetic and copies ran while one was open for 30% of the time, Pallas kernels for 10%

commit v1 on v0

--- a/solution.py
+++ b/solution.py
@@ -128,6 +128,56 @@
     )(qkv, bias)
 
 
+def fine_mlp_kernel(tokens_ref, attended_ref, out_ref, up_ref, down_ref, skip_ref, stream_ref, normed_ref):
+    step = pl.program_id(0)
+
+    @pl.when(step == 0)
+    def _():
+        stream = tokens_ref[...].astype(jnp.float32) + jnp.dot(
+            attended_ref[...], out_ref[...], preferred_element_type=jnp.float32
+        )
+        stream_ref[...] = stream
+        normed_ref[...] = layer_norm(stream).astype(jnp.bfloat16)
+
+    wide = jnp.dot(normed_ref[...], up_ref[...], preferred_element_type=jnp.float32)
+    hidden = (0.5 * wide * (1.0 + lax.erf(wide * 0.5**0.5))).astype(jnp.bfloat16)
+    stream_ref[...] += jnp.dot(hidden, down_ref[...], preferred_element_type=jnp.float32)
+
+    @pl.when(step == pl.num_programs(0) - 1)
+    def _():
+        skip_ref[...] = stream_ref[...].astype(jnp.bfloat16)
+
+
+def fine_mlp(tokens, attended, out, up, down):
+    count, width = tokens.shape
+    hidden = up.shape[1]
+    tile = 512
+    whole = pl.BlockSpec((count, width), lambda s: (0, 0))
+    return pl.pallas_call(
+        fine_mlp_kernel,
+        out_shape=jax.ShapeDtypeStruct((count, width), jnp.bfloat16),
+        grid=(hidden // tile,),
+        in_specs=[
+            whole,
+            whole,
+            pl.BlockSpec((width, width), lambda s: (0, 0)),
+            pl.BlockSpec((width, tile), lambda s: (0, s)),
+            pl.BlockSpec((tile, width), lambda s: (s, 0)),
+        ],
+        out_specs=whole,
+        scratch_shapes=[
+            pltpu.VMEM((count, width), jnp.float32),
+            pltpu.VMEM((count, width), jnp.bfloat16),
+        ],
+        compiler_params=pltpu.CompilerParams(vmem_limit_bytes=32 * 2**20),
+        cost_estimate=pl.CostEstimate(
+            flops=2 * count * width * (width + 2 * hidden),
+            bytes_accessed=2 * width * (width + 2 * hidden),
+            transcendentals=count * hidden,
+        ),
+    )(tokens, attended, out, up, down)
+
+
 def coarse_attend_kernel(x_ref, qkv_ref, rows_ref, a0_ref, a1_ref, b0_ref, b1_ref, own_ref, peer_ref, sum_ref):
     lat = lax.axis_index("lat")
     count, width = x_ref.shape
@@ -244,12 +294,12 @@
     return lax.ppermute(block, axis, [(i, i ^ bit) for i in range(lax.axis_size(axis))])
 
 
-def along_lon(a, b):
+def along_lon(a, b, shifts):
     lons = lax.axis_size("lon")
     both = jnp.stack([a, b])
     return [
         lax.ppermute(both, "lon", [(i, (i + shift) % lons) for i in range(lons)])
-        for shift in range(2, lons, 2)
+        for shift in shifts
     ]
 
 
@@ -275,7 +325,7 @@
     return (first, second), (up, lax.dynamic_slice_in_dim(down, lat * BLK, BLK, 1))
 
 
-def local_level(tokens, attend_moved, mlp_moved, qkv, out, up, down):
+def local_level(tokens, attend_moved, near, middle, far, qkv, out, up, down):
     count = tokens.shape[0]
 
     def shared(values):
@@ -283,10 +333,15 @@
         return jnp.concatenate([normed, swapped(normed, "lon", 1)], axis=0)
 
     own, peer = coarse_attend(shared(tokens), qkv, out, attend_moved)
+    peer, far, middle = lax.optimization_barrier((peer, far, middle))
+    middle = first_swap([middle])
+    far = second_swap(*far)
     tokens = tokens + own + swapped(peer, "lon", 1).astype(jnp.float32)
     both = shared(tokens)
+    both, middle = lax.optimization_barrier((both, middle))
+    middle = second_swap(*middle)
     total = own_mlp(both, up, down)
-    for moved in mlp_moved:
+    for moved in (near, far, middle):
         total = moved_mlp(both, total, moved)
     peer = swapped(total[count:].astype(jnp.bfloat16), "lon", 1)
     return (tokens + total[:count] + peer.astype(jnp.float32)).astype(jnp.bfloat16)
@@ -313,12 +368,12 @@
     )
     if whole_weights:
         attend_part, mlp_part = level_parts(coarse_qkv, coarse_out, coarse_up, coarse_down)
-        attend_moved, mlp_moved = (along_lon(*attend_part), along_lon(*mlp_part))
-    stream = tokens.astype(jnp.float32)
-    normed = layer_norm(stream).astype(jnp.bfloat16)
-    below_rows = shifted_2(normed[:SH], "lat", -1)
-    shifted = jnp.concatenate([normed[SH:], below_rows], axis=0)
+    below_rows = shifted_2(tokens[:SH], "lat", -1)
+    shifted = jnp.concatenate([tokens[SH:], below_rows], axis=0)
     east_cols = shifted_2(shifted[:, :SW], "lon", -1)
+    if whole_weights:
+        east_cols, attend_part, mlp_part = lax.optimization_barrier((east_cols, attend_part, mlp_part))
+        attend_moved = along_lon(*attend_part, (2, 4, 6))
     shifted = jnp.concatenate([shifted[:, SW:], east_cols], axis=1)
     anchor = (lat_index * band_rows + jnp.arange(band_rows, dtype=jnp.int32) + SH) % total_rows
     labels = (anchor < SH).astype(jnp.int32)
@@ -331,16 +386,16 @@
         .transpose(0, 2, 1, 3, 4)
         .reshape(row_wins * col_wins, WH * WW, -1)
     )
-    packed = project(shifted, fine_qkv).astype(jnp.bfloat16)
-    if whole_weights:
-        packed, attend_moved = lax.optimization_barrier((packed, attend_moved))
+    shifted = lax.optimization_barrier(shifted)
+    normed = layer_norm(shifted.astype(jnp.float32)).astype(jnp.bfloat16)
+    packed = project(normed, fine_qkv).astype(jnp.bfloat16)
+    if whole_weights:
+        packed, mlp_part = lax.optimization_barrier((packed, mlp_part))
+        (near,) = along_lon(*mlp_part, (2,))
+    attended = fine_attend(packed, bias)
+    if whole_weights:
+        attended, attend_moved = lax.optimization_barrier((attended, attend_moved))
         attend_moved = first_swap(attend_moved)
-    attended = fine_attend(packed, bias)
-    if whole_weights:
-        near, middle, far = mlp_moved
-        attended, attend_moved, near = lax.optimization_barrier((attended, attend_moved, near))
-        attend_moved = second_swap(*attend_moved)
-        near = first_swap([near])
     attended = (
         attended.reshape(row_wins, col_wins, WH, WW, -1)
         .transpose(0, 2, 1, 3, 4)
@@ -351,19 +406,20 @@
     west_cols = shifted_2(attended[:, band_cols - SW :], "lon", 1)
     attended = jnp.concatenate([west_cols, attended[:, : band_cols - SW]], axis=1)
     if whole_weights:
-        attended, near, far = lax.optimization_barrier((attended, near, far))
-        far = first_swap([far])
-        near = second_swap(*near)
-    stream = stream + project(attended, fine_out)
-    hidden = jax.nn.gelu(
-        project(layer_norm(stream).astype(jnp.bfloat16), fine_up), approximate=False
-    ).astype(jnp.bfloat16)
-    if whole_weights:
-        hidden, far, middle = lax.optimization_barrier((hidden, far, middle))
-        middle = first_swap([middle])
-        far = second_swap(*far)
-    skip_tokens = (stream + project(hidden, fine_down)).astype(jnp.bfloat16)
-    skip_tokens = lax.optimization_barrier(skip_tokens)
+        attended, attend_moved, mlp_part = lax.optimization_barrier((attended, attend_moved, mlp_part))
+        far, middle = along_lon(*mlp_part, (6, 4))
+        attend_moved = second_swap(*attend_moved)
+    skip_tokens = fine_mlp(
+        tokens.reshape(band_rows * band_cols, -1),
+        attended.reshape(band_rows * band_cols, -1),
+        fine_out,
+        fine_up,
+        fine_down,
+    )
+    if whole_weights:
+        skip_tokens, near = lax.optimization_barrier((skip_tokens, near))
+        near = first_swap([near])
+    skip_tokens = lax.optimization_barrier(skip_tokens).reshape(tokens.shape)
     coarse_rows, coarse_cols = (band_rows // 2, band_cols // 2)
     wins = (coarse_rows // WH, WH, 2, coarse_cols // WW, WW, 2)
     merged = (
@@ -377,10 +433,11 @@
     ).astype(jnp.bfloat16)
     coarse_float = coarse.astype(jnp.float32)
     if whole_weights:
-        coarse_float, middle = lax.optimization_barrier((coarse_float, middle))
-        mlp_moved = (near, far, second_swap(*middle))
+        coarse_float, near, far = lax.optimization_barrier((coarse_float, near, far))
+        far = first_swap([far])
+        near = second_swap(*near)
         level_state = local_level(
-            coarse_float, attend_moved, mlp_moved, coarse_qkv, coarse_out, coarse_up, coarse_down
+            coarse_float, attend_moved, near, middle, far, coarse_qkv, coarse_out, coarse_up, coarse_down
         )
     else:
         coarse_float = (

time: 183 us -> 157 us (0.86)
  the two profiles are of different devices: /device:TPU:21 before, /device:TPU:1 now
where the time goes in v1:
time: 157 us; the launch traced here: 155 us
  starting transfers between devices  50 us (32%)
  waiting for transfers between devices  35.3 us (22%)
  local copies, waits for them, and re-layouts  29.4 us (19%)
  Pallas kernels  23.3 us (15%)
  other arithmetic  13 us (8%)
  matrix products  3.68 us (2%)
    ppermute x20, starting transfers between devices, swapped(): lax.ppermute(block, axis, [(i, i ^ bit) for i in range(lax.axis_size(axis...  28.8 us
    ppermute x20, waiting for transfers between devices, swapped(): lax.ppermute(block, axis, [(i, i ^ bit) for i in range(lax.axis_size(axis...  27.8 us
    ppermute x6, starting transfers between devices, along_lon(): lax.ppermute(both, 'lon', [(i, (i + shift) % lons) for i in range(lons)])  11.2 us
    ppermute x4, starting transfers between devices, shifted_2(): return lax.ppermute(block, axis, route)  9.99 us
    pallas_call x1, Pallas kernels, fine_attend(): pl.pallas_call(functools.partial(fine_kernel, width // (3 * HD)), out_sha...  8.44 us
    pallas_call x1, Pallas kernels, coarse_attend(): pl.pallas_call(coarse_attend_kernel, out_shape=(jax.ShapeDtypeStruct((cou...  6.71 us
    slice x6, local copies, waits for them, and re-layouts, first_swap(): b = jnp.stack([one[1] for one in got])  6.31 us
    ppermute x4, waiting for transfers between devices, shifted_2(): return lax.ppermute(block, axis, route)  4.81 us
  transfers between devices with their start and end apart: 30, of which 13 were waited for; matrix products, arithmetic and copies ran while one was open for 20% of the time, Pallas kernels for 14%

profile of v1, /device:TPU:1, one launch (start us, length us, event | category | flops | bytes accessed | tf_op | source)
XLA Modules:
  0.0 155.5 jit_solution(13118222320746738798)
XLA Ops:
  0.0 1.7 %slice.77 = bf16[3,48,512]{2,1,0:T(8,128)(2,1)} slice(bf16[12,48,512]{2,1,0:T(8,128)(2,1)} %param.11), slice={[0:3], [0:48], [0:512]} | slice | bytes 294912 | tf_op jit(solution)/shard_map/slice | solution.py:371
  1.7 3.0 %collective-permute-start = (bf16[3,48,512]{2,1,0:T(8,128)(2,1)}, bf16[3,48,512]{2,1,0:T(8,128)(2,1)}, u32[]{:S(2)}, u32[]{:S(2)}) collective-permute-start(bf16[3,48,512]{2,1,0:T(8,128)(2,1)} %slice.77), channel_id=1, source_target_pairs={{8,0},{16,8},{24,16},{0,24},{9,1},{17,9},{25,17},{1,25},{10,2},{18... | collective-permute-start | bytes 442376 | tf_op jit(solution)/shard_map/ppermute | solution.py:20
  8.3 1.7 %constant_dynamic-slice_fusion.1 = (bf16[1024,128]{1,0:T(8,128)(2,1)S(1)}, bf16[1024,128]{1,0:T(8,128)(2,1)}) fusion(bf16[1024,512]{1,0:T(8,128)(2,1)} %refs_1_.1, s32[]{:T(128)S(6)} %select_n.21, bf16[1024,512]{1,0:T(8,128)(2,1)S(1)} %copy-done.2), kind=kLoop, calls=%fused_computation.75 | loop fusion | bytes 1048580 | tf_op jit(solution)/shard_map/dynamic_slice | solution.py:325
  12.9 2.4 %collective-permute-done.1 = bf16[12,6,512]{2,1,0:T(8,128)(2,1)S(1)} collective-permute-done((bf16[12,6,512]{2,1,0:T(8,128)(2,1)S(1)}, bf16[12,6,512]{2,1,0:T(8,128)(2,1)S(1)}, u32[]{:S(2)}, u32[]{:S(2)}) %collective-permute-start.1) | collective-permute-done | bytes 73760 | tf_op jit(solution)/shard_map/ppermute | solution.py:20
  17.3 3.7 %collective-permute-start.3 = (bf16[2,512,128]{2,1,0:T(8,128)(2,1)}, bf16[2,512,128]{2,1,0:T(8,128)(2,1)}, u32[]{:S(2)}, u32[]{:S(2)}) collective-permute-start(bf16[2,512,128]{2,1,0:T(8,128)(2,1)} %pad_maximum_fusion.8), channel_id=1, source_target_pairs={{0,4},{1,5},{2,6},{3,7},{4,0},{5,1},{6,2},{7,3},{8,12},{9,13},{10,... | collective-permute-start | bytes 786440 | tf_op jit(solution)/shard_map/ppermute | solution.py:301
  22.1 2.4 %copy.32 = bf16[2,4,6,12,512]{4,1,0,3,2:T(4,128)(2,1)} copy(bf16[2,4,6,12,512]{4,3,1,2,0:T(8,128)(2,1)} %bitcast.31) | data formatting | bytes 1179648 | tf_op jit(solution)/shard_map/transpose | solution.py:386
  27.9 8.4 %shard_map.109 = bf16[8,72,512]{2,1,0:T(8,128)(2,1)S(1)} custom-call(bf16[8,72,1536]{2,1,0:T(8,128)(2,1)S(1)} %convolution_convert_fusion.qkv_ref, f32[2,72,72]{2,1,0:T(8,128)S(1)} %compare_select_fusion.bias_ref), custom_call_target="tpu_custom_call" | custom-call | flops 84934656 | bytes 2654208 | tf_op jit(solution)/shard_map/pallas_call | solution.py:113
  36.3 2.6 %collective-permute-done.3 = bf16[2,512,128]{2,1,0:T(8,128)(2,1)} collective-permute-done((bf16[2,512,128]{2,1,0:T(8,128)(2,1)}, bf16[2,512,128]{2,1,0:T(8,128)(2,1)}, u32[]{:S(2)}, u32[]{:S(2)}) %collective-permute-start.3) | collective-permute-done | bytes 262176 | tf_op jit(solution)/shard_map/ppermute | solution.py:301
  46.3 6.0 %collective-permute-start.6 = (bf16[12,6,512]{2,1,0:T(8,128)(2,1)S(1)}, bf16[12,6,512]{2,1,0:T(8,128)(2,1)S(1)}, u32[]{:S(2)}, u32[]{:S(2)}) collective-permute-start(bf16[12,6,512]{2,1,0:T(8,128)(2,1)S(1)} %pad_maximum_fusion.11), channel_id=1, source_target_pairs={{7,0},{0,1},{1,2},{2,3},{3,4},{4,5},{5,6},{6,7},{15,8},{8,9},{9,10... | collective-permute-start | bytes 221192 | tf_op jit(solution)/shard_map/ppermute | solution.py:20
  52.4 1.8 %collective-permute-done.6 = bf16[12,6,512]{2,1,0:T(8,128)(2,1)S(1)} collective-permute-done((bf16[12,6,512]{2,1,0:T(8,128)(2,1)S(1)}, bf16[12,6,512]{2,1,0:T(8,128)(2,1)S(1)}, u32[]{:S(2)}, u32[]{:S(2)}) %collective-permute-start.6) | collective-permute-done | bytes 73760 | tf_op jit(solution)/shard_map/ppermute | solution.py:20
  55.8 4.5 %collective-permute-start.12 = (bf16[2,1024,128]{2,1,0:T(8,128)(2,1)}, bf16[2,1024,128]{2,1,0:T(8,128)(2,1)}, u32[]{:S(2)}, u32[]{:S(2)}) collective-permute-start(bf16[2,1024,128]{2,1,0:T(8,128)(2,1)} %pad_maximum_fusion.5), channel_id=1, source_target_pairs={{0,6},{1,7},{2,0},{3,1},{4,2},{5,3},{6,4},{7,5},{8,14},{9,15},{10,... | collective-permute-start | bytes 1572872 | tf_op jit(solution)/shard_map/ppermute | solution.py:301
  60.3 1.6 %collective-permute-start.18 = (bf16[2,1024,128]{2,1,0:T(8,128)(2,1)}, bf16[2,1024,128]{2,1,0:T(8,128)(2,1)}, u32[]{:S(2)}, u32[]{:S(2)}) collective-permute-start(bf16[2,1024,128]{2,1,0:T(8,128)(2,1)} %pad_maximum_fusion.5), channel_id=1, source_target_pairs={{0,4},{1,5},{2,6},{3,7},{4,0},{5,1},{6,2},{7,3},{8,12},{9,13},{10,... | collective-permute-start | bytes 1572872 | tf_op jit(solution)/shard_map/ppermute | solution.py:301
  61.9 4.6 %shard_map.110 = bf16[576,512]{1,0:T(8,128)(2,1)S(1)} custom-call(bf16[576,512]{1,0:T(8,128)(2,1)S(1)} %bitcast.29, bf16[576,512]{1,0:T(8,128)(2,1)S(1)} %bitcast.28, bf16[512,512]{1,0:T(8,128)(2,1)S(1)} %copy-done.10, bf16[512,2048]{1,0:T(8,128)(2,1)S(1)} %copy-done.8, bf16[2048,512]{1,0:T(8,128)(2,1)S(1)} %copy-done.9), custom_call_target="tpu_custom_call" | custom-call | flops 2717908992 | bytes 4718592 | tf_op jit(solution)/shard_map/pallas_call | solution.py:156
  73.6 1.7 %fusion.5 = f32[144,1024]{1,0:T(8,128)} fusion(bf16[2048,1024]{1,0:T(8,128)(2,1)S(1)} %copy-done.14, bf16[144,2048]{1,0:T(8,128)(2,1)S(1)} %copy-done.13, f32[144]{0:T(256)S(1)} %add_rsqrt_fusion.4, f32[144]{0:T(256)S(1)} %broadcast_multiply_fusion.4), kind=kOutput, calls=%fused_computation.11 | convolution fusion | flops 605454336 | bytes 5375104 | tf_op jit(solution)/shard_map/dot_general | solution.py:32
  80.9 4.9 %collective-permute-start.13 = (bf16[144,1024]{1,0:T(8,128)(2,1)S(1)}, bf16[144,1024]{1,0:T(8,128)(2,1)S(1)}, u32[]{:S(2)}, u32[]{:S(2)}) collective-permute-start(bf16[144,1024]{1,0:T(8,128)(2,1)S(1)} %multiply_convert_fusion.1), channel_id=1, source_target_pairs={{0,1},{1,0},{2,3},{3,2},{4,5},{5,4},{6,7},{7,6},{8,9},{9,8},{10,11... | collective-permute-start | bytes 884744 | tf_op jit(solution)/shard_map/ppermute | solution.py:294
  89.8 2.8 %collective-permute-done.14.a1_ref = bf16[6,512,128]{2,1,0:T(8,128)(2,1)} collective-permute-done((bf16[6,512,128]{2,1,0:T(8,128)(2,1)S(1)}, bf16[6,512,128]{2,1,0:T(8,128)(2,1)}, u32[]{:S(2)}, u32[]{:S(2)}) %collective-permute-start.14) | collective-permute-done | bytes 786464 | tf_op jit(solution)/shard_map/ppermute | solution.py:294
  94.6 6.7 %shard_map.111 = (f32[144,1024]{1,0:T(8,128)S(1)}, bf16[144,1024]{1,0:T(8,128)(2,1)S(1)}) custom-call(bf16[288,1024]{1,0:T(8,128)(2,1)S(1)} %pad_maximum_fusion.2.x_ref, bf16[1024,384]{1,0:T(8,128)(2,1)S(1)} %copy-done.4, bf16[1024,128]{1,0:T(8,128)(2,1)S(1)} %copy-done.7, bf16[6,512,128]{2,1,0:T(8,128)(2,1)S(1)} %constant_dynamic-update-slice_fusion.a0_ref, ...), custom_call_target="tpu_custom_call" | custom-call | flops 1207959552 | bytes 4194304 | tf_op jit(solution)/shard_map/pallas_call | solution.py:226
  101.3 6.9 %collective-permute-start.19 = (bf16[144,1024]{1,0:T(8,128)(2,1)S(1)}, bf16[144,1024]{1,0:T(8,128)(2,1)S(1)}, u32[]{:S(2)}, u32[]{:S(2)}) collective-permute-start(bf16[144,1024]{1,0:T(8,128)(2,1)S(1)} %get-tuple-element.70), channel_id=1, source_target_pairs={{0,1},{1,0},{2,3},{3,2},{4,5},{5,4},{6,7},{7,6},{8,9},{9,8},{10,11... | collective-permute-start | bytes 884744 | tf_op jit(solution)/shard_map/ppermute | solution.py:294
  113.4 3.8 %collective-permute-done.21 = bf16[1,1024,128]{2,1,0:T(8,128)(2,1)S(1)} collective-permute-done((bf16[1,1024,128]{2,1,0:T(8,128)(2,1)S(1)}, bf16[1,1024,128]{2,1,0:T(8,128)(2,1)S(1)}, u32[]{:S(2)}, u32[]{:S(2)}) %collective-permute-start.21) | collective-permute-done | bytes 262176 | tf_op jit(solution)/shard_map/ppermute | solution.py:294
  121.7 6.6 %collective-permute-done.25.refs_2_.refs_3_ = bf16[2,1024,128]{2,1,0:T(8,128)(2,1)S(1)} collective-permute-done((bf16[2,1024,128]{2,1,0:T(8,128)(2,1)S(1)}, bf16[2,1024,128]{2,1,0:T(8,128)(2,1)S(1)}, u32[]{:S(2)}, u32[]{:S(2)}) %collective-permute-start.25) | collective-permute-done | bytes 524320 | tf_op jit(solution)/shard_map/ppermute | solution.py:294
  130.7 8.8 %collective-permute-done.27.refs_2_.refs_3_ = bf16[2,1024,128]{2,1,0:T(8,128)(2,1)S(1)} collective-permute-done((bf16[2,1024,128]{2,1,0:T(8,128)(2,1)S(1)}, bf16[2,1024,128]{2,1,0:T(8,128)(2,1)S(1)}, u32[]{:S(2)}, u32[]{:S(2)}) %collective-permute-start.27) | collective-permute-done | bytes 524320 | tf_op jit(solution)/shard_map/ppermute | solution.py:294
  142.0 1.8 %collective-permute-start.29 = (bf16[144,1024]{1,0:T(8,128)(2,1)S(1)}, bf16[144,1024]{1,0:T(8,128)(2,1)S(1)}, u32[]{:S(2)}, u32[]{:S(2)}) collective-permute-start(bf16[144,1024]{1,0:T(8,128)(2,1)S(1)} %slice.116), channel_id=1, source_target_pairs={{0,1},{1,0},{2,3},{3,2},{4,5},{5,4},{6,7},{7,6},{8,9},{9,8},{10,11... | collective-permute-start | bytes 884744 | tf_op jit(solution)/shard_map/ppermute | solution.py:294
  148.3 1.6 %copy.37 = f32[1,6,2,2,12,2,512]{6,5,4,3,2,1,0:T(2,128)} copy(f32[1,6,2,2,12,2,512]{6,5,2,4,1,3,0:T(2,128)S(1)} %bitcast.30) | data formatting | bytes 2359296 | tf_op jit(solution)/shard_map/transpose | solution.py:476
  149.9 2.1 %reshape.123 = f32[12,48,512]{2,1,0:T(8,128)S(1)} reshape(f32[1,6,2,2,12,2,512]{6,5,4,3,2,1,0:T(2,128)} %copy.37) | data formatting | bytes 2359296 | tf_op jit(solution)/shard_map/reshape | solution.py:477
  (202 shorter events, 62.5 us)
Async XLA Ops:
  1.7 8.3 %collective-permute-start = (bf16[3,48,512]{2,1,0:T(8,128)(2,1)}, bf16[3,48,512]{2,1,0:T(8,128)(2,1)}, u32[]{:S(2)}, u32[]{:S(2)}) collective-permute-start(bf16[3,48,512]{2,1,0:T(8,128)(2,1)} %slice.77), channel_id=1, source_target_pairs={{8,0},{16,8},{24,16},{0,24},{9,1},{17,9},{25,17},{1,25},{10,2},{18... | collective-permute-start | bytes 442376 | tf_op jit(solution)/shard_map/ppermute | solution.py:20
  16.0 20.3 %collective-permute-start.2 = (bf16[2,512,128]{2,1,0:T(8,128)(2,1)}, bf16[2,512,128]{2,1,0:T(8,128)(2,1)}, u32[]{:S(2)}, u32[]{:S(2)}) collective-permute-start(bf16[2,512,128]{2,1,0:T(8,128)(2,1)} %pad_maximum_fusion.8), channel_id=1, source_target_pairs={{0,2},{1,3},{2,4},{3,5},{4,6},{5,7},{6,0},{7,1},{8,10},{9,11},{10,... | collective-permute-start | bytes 786440 | tf_op jit(solution)/shard_map/ppermute | solution.py:301
  17.3 21.7 %collective-permute-start.3 = (bf16[2,512,128]{2,1,0:T(8,128)(2,1)}, bf16[2,512,128]{2,1,0:T(8,128)(2,1)}, u32[]{:S(2)}, u32[]{:S(2)}) collective-permute-start(bf16[2,512,128]{2,1,0:T(8,128)(2,1)} %pad_maximum_fusion.8), channel_id=1, source_target_pairs={{0,4},{1,5},{2,6},{3,7},{4,0},{5,1},{6,2},{7,3},{8,12},{9,13},{10,... | collective-permute-start | bytes 786440 | tf_op jit(solution)/shard_map/ppermute | solution.py:301
  21.0 17.9 %collective-permute-start.4 = (bf16[2,512,128]{2,1,0:T(8,128)(2,1)}, bf16[2,512,128]{2,1,0:T(8,128)(2,1)}, u32[]{:S(2)}, u32[]{:S(2)}) collective-permute-start(bf16[2,512,128]{2,1,0:T(8,128)(2,1)} %pad_maximum_fusion.8), channel_id=1, source_target_pairs={{0,6},{1,7},{2,0},{3,1},{4,2},{5,3},{6,4},{7,5},{8,14},{9,15},{10,... | collective-permute-start | bytes 786440 | tf_op jit(solution)/shard_map/ppermute | solution.py:301
  42.8 11.6 %collective-permute-start.7 = (bf16[3,512,128]{2,1,0:T(8,128)(2,1)S(1)}, bf16[3,512,128]{2,1,0:T(8,128)(2,1)S(1)}, u32[]{:S(2)}, u32[]{:S(2)}) collective-permute-start(bf16[3,512,128]{2,1,0:T(8,128)(2,1)S(1)} %pad_maximum_fusion.6), channel_id=1, source_target_pairs={{0,8},{8,0},{16,24},{24,16},{1,9},{9,1},{17,25},{25,17},{2,10},{10... | collective-permute-start | bytes 1179656 | tf_op jit(solution)/shard_map/ppermute | solution.py:294
  44.3 10.6 %collective-permute-start.8 = (bf16[3,512,128]{2,1,0:T(8,128)(2,1)S(1)}, bf16[3,512,128]{2,1,0:T(8,128)(2,1)S(1)}, u32[]{:S(2)}, u32[]{:S(2)}) collective-permute-start(bf16[3,512,128]{2,1,0:T(8,128)(2,1)S(1)} %pad_maximum_fusion.7), channel_id=1, source_target_pairs={{0,16},{8,24},{16,0},{24,8},{1,17},{9,25},{17,1},{25,9},{2,18},{10... | collective-permute-start | bytes 1179656 | tf_op jit(solution)/shard_map/ppermute | solution.py:294
  46.3 7.9 %collective-permute-start.6 = (bf16[12,6,512]{2,1,0:T(8,128)(2,1)S(1)}, bf16[12,6,512]{2,1,0:T(8,128)(2,1)S(1)}, u32[]{:S(2)}, u32[]{:S(2)}) collective-permute-start(bf16[12,6,512]{2,1,0:T(8,128)(2,1)S(1)} %pad_maximum_fusion.11), channel_id=1, source_target_pairs={{7,0},{0,1},{1,2},{2,3},{3,4},{4,5},{5,6},{6,7},{15,8},{8,9},{9,10... | collective-permute-start | bytes 221192 | tf_op jit(solution)/shard_map/ppermute | solution.py:20
  52.4 14.1 %collective-permute-start.9 = (bf16[2,1024,128]{2,1,0:T(8,128)(2,1)S(1)}, bf16[2,1024,128]{2,1,0:T(8,128)(2,1)}, u32[]{:S(2)}, u32[]{:S(2)}) collective-permute-start(bf16[2,1024,128]{2,1,0:T(8,128)(2,1)S(1)} %pad_maximum_fusion.4), channel_id=1, source_target_pairs={{0,2},{1,3},{2,4},{3,5},{4,6},{5,7},{6,0},{7,1},{8,10},{9,11},{10,... | collective-permute-start | bytes 1572872 | tf_op jit(solution)/shard_map/ppermute | solution.py:301
  55.8 21.3 %collective-permute-start.12 = (bf16[2,1024,128]{2,1,0:T(8,128)(2,1)}, bf16[2,1024,128]{2,1,0:T(8,128)(2,1)}, u32[]{:S(2)}, u32[]{:S(2)}) collective-permute-start(bf16[2,1024,128]{2,1,0:T(8,128)(2,1)} %pad_maximum_fusion.5), channel_id=1, source_target_pairs={{0,6},{1,7},{2,0},{3,1},{4,2},{5,3},{6,4},{7,5},{8,14},{9,15},{10,... | collective-permute-start | bytes 1572872 | tf_op jit(solution)/shard_map/ppermute | solution.py:301
  60.3 41.0 %collective-permute-start.18 = (bf16[2,1024,128]{2,1,0:T(8,128)(2,1)}, bf16[2,1024,128]{2,1,0:T(8,128)(2,1)}, u32[]{:S(2)}, u32[]{:S(2)}) collective-permute-start(bf16[2,1024,128]{2,1,0:T(8,128)(2,1)} %pad_maximum_fusion.5), channel_id=1, source_target_pairs={{0,4},{1,5},{2,6},{3,7},{4,0},{5,1},{6,2},{7,3},{8,12},{9,13},{10,... | collective-permute-start | bytes 1572872 | tf_op jit(solution)/shard_map/ppermute | solution.py:301
  71.2 21.3 %collective-permute-start.14 = (bf16[6,512,128]{2,1,0:T(8,128)(2,1)S(1)}, bf16[6,512,128]{2,1,0:T(8,128)(2,1)}, u32[]{:S(2)}, u32[]{:S(2)}) collective-permute-start(bf16[6,512,128]{2,1,0:T(8,128)(2,1)S(1)} %constant_dynamic-update-slice_fusion.a0_ref), channel_id=1, source_target_pairs={{0,16},{8,24},{16,0},{24,8},{1,17},{9,25},{17,1},{25,9},{2,18},{10... | collective-permute-start | bytes 2359304 | tf_op jit(solution)/shard_map/ppermute | solution.py:294
  75.3 18.5 %collective-permute-start.15 = (bf16[6,512,128]{2,1,0:T(8,128)(2,1)S(1)}, bf16[6,512,128]{2,1,0:T(8,128)(2,1)}, u32[]{:S(2)}, u32[]{:S(2)}) collective-permute-start(bf16[6,512,128]{2,1,0:T(8,128)(2,1)S(1)} %constant_dynamic-update-slice_fusion.2.b0_ref), channel_id=1, source_target_pairs={{0,8},{8,0},{16,24},{24,16},{1,9},{9,1},{17,25},{25,17},{2,10},{10... | collective-permute-start | bytes 2359304 | tf_op jit(solution)/shard_map/ppermute | solution.py:294
  80.9 7.5 %collective-permute-start.13 = (bf16[144,1024]{1,0:T(8,128)(2,1)S(1)}, bf16[144,1024]{1,0:T(8,128)(2,1)S(1)}, u32[]{:S(2)}, u32[]{:S(2)}) collective-permute-start(bf16[144,1024]{1,0:T(8,128)(2,1)S(1)} %multiply_convert_fusion.1), channel_id=1, source_target_pairs={{0,1},{1,0},{2,3},{3,2},{4,5},{5,4},{6,7},{7,6},{8,9},{9,8},{10,11... | collective-permute-start | bytes 884744 | tf_op jit(solution)/shard_map/ppermute | solution.py:294
  86.8 14.5 %collective-permute-start.16 = (bf16[1,1024,128]{2,1,0:T(8,128)(2,1)S(1)}, bf16[1,1024,128]{2,1,0:T(8,128)(2,1)S(1)}, u32[]{:S(2)}, u32[]{:S(2)}) collective-permute-start(bf16[1,1024,128]{2,1,0:T(8,128)(2,1)S(1)} %get-tuple-element.77), channel_id=1, source_target_pairs={{0,8},{8,0},{16,24},{24,16},{1,9},{9,1},{17,25},{25,17},{2,10},{10... | collective-permute-start | bytes 786440 | tf_op jit(solution)/shard_map/ppermute | solution.py:294
  88.4 12.9 %collective-permute-start.17 = (bf16[1,1024,128]{2,1,0:T(8,128)(2,1)S(1)}, bf16[1,1024,128]{2,1,0:T(8,128)(2,1)S(1)}, u32[]{:S(2)}, u32[]{:S(2)}) collective-permute-start(bf16[1,1024,128]{2,1,0:T(8,128)(2,1)S(1)} %get-tuple-element.79), channel_id=1, source_target_pairs={{0,16},{8,24},{16,0},{24,8},{1,17},{9,25},{17,1},{25,9},{2,18},{10... | collective-permute-start | bytes 786440 | tf_op jit(solution)/shard_map/ppermute | solution.py:294
  92.6 25.8 %collective-permute-start.23 = (bf16[2,1024,128]{2,1,0:T(8,128)(2,1)S(1)}, bf16[2,1024,128]{2,1,0:T(8,128)(2,1)S(1)}, u32[]{:S(2)}, u32[]{:S(2)}) collective-permute-start(bf16[2,1024,128]{2,1,0:T(8,128)(2,1)S(1)} %constant_dynamic-update-slice_fusion.4.refs_0_.refs_1_), channel_id=1, source_target_pairs={{0,16},{8,24},{16,0},{24,8},{1,17},{9,25},{17,1},{25,9},{2,18},{10... | collective-permute-start | bytes 1572872 | tf_op jit(solution)/shard_map/ppermute | solution.py:294
  93.8 27.0 %collective-permute-start.24 = (bf16[2,1024,128]{2,1,0:T(8,128)(2,1)S(1)}, bf16[2,1024,128]{2,1,0:T(8,128)(2,1)S(1)}, u32[]{:S(2)}, u32[]{:S(2)}) collective-permute-start(bf16[2,1024,128]{2,1,0:T(8,128)(2,1)S(1)} %constant_dynamic-update-slice_fusion.6.refs_4_.refs_6_), channel_id=1, source_target_pairs={{0,8},{8,0},{16,24},{24,16},{1,9},{9,1},{17,25},{25,17},{2,10},{10... | collective-permute-start | bytes 1572872 | tf_op jit(solution)/shard_map/ppermute | solution.py:294
  101.3 8.5 %collective-permute-start.19 = (bf16[144,1024]{1,0:T(8,128)(2,1)S(1)}, bf16[144,1024]{1,0:T(8,128)(2,1)S(1)}, u32[]{:S(2)}, u32[]{:S(2)}) collective-permute-start(bf16[144,1024]{1,0:T(8,128)(2,1)S(1)} %get-tuple-element.70), channel_id=1, source_target_pairs={{0,1},{1,0},{2,3},{3,2},{4,5},{5,4},{6,7},{7,6},{8,9},{9,8},{10,11... | collective-permute-start | bytes 884744 | tf_op jit(solution)/shard_map/ppermute | solution.py:294
  109.3 7.9 %collective-permute-start.21 = (bf16[1,1024,128]{2,1,0:T(8,128)(2,1)S(1)}, bf16[1,1024,128]{2,1,0:T(8,128)(2,1)S(1)}, u32[]{:S(2)}, u32[]{:S(2)}) collective-permute-start(bf16[1,1024,128]{2,1,0:T(8,128)(2,1)S(1)} %get-tuple-element.81), channel_id=1, source_target_pairs={{0,8},{8,0},{16,24},{24,16},{1,9},{9,1},{17,25},{25,17},{2,10},{10... | collective-permute-start | bytes 786440 | tf_op jit(solution)/shard_map/ppermute | solution.py:294
  109.4 8.4 %collective-permute-start.22 = (bf16[1,1024,128]{2,1,0:T(8,128)(2,1)S(1)}, bf16[1,1024,128]{2,1,0:T(8,128)(2,1)S(1)}, u32[]{:S(2)}, u32[]{:S(2)}) collective-permute-start(bf16[1,1024,128]{2,1,0:T(8,128)(2,1)S(1)} %get-tuple-element.83), channel_id=1, source_target_pairs={{0,16},{8,24},{16,0},{24,8},{1,17},{9,25},{17,1},{25,9},{2,18},{10... | collective-permute-start | bytes 786440 | tf_op jit(solution)/shard_map/ppermute | solution.py:294
  112.3 16.0 %collective-permute-start.25 = (bf16[2,1024,128]{2,1,0:T(8,128)(2,1)S(1)}, bf16[2,1024,128]{2,1,0:T(8,128)(2,1)S(1)}, u32[]{:S(2)}, u32[]{:S(2)}) collective-permute-start(bf16[2,1024,128]{2,1,0:T(8,128)(2,1)S(1)} %constant_dynamic-update-slice_fusion.8.refs_0_.refs_1_), channel_id=1, source_target_pairs={{0,16},{8,24},{16,0},{24,8},{1,17},{9,25},{17,1},{25,9},{2,18},{10... | collective-permute-start | bytes 1572872 | tf_op jit(solution)/shard_map/ppermute | solution.py:294
  117.2 12.6 %collective-permute-start.26 = (bf16[2,1024,128]{2,1,0:T(8,128)(2,1)S(1)}, bf16[2,1024,128]{2,1,0:T(8,128)(2,1)S(1)}, u32[]{:S(2)}, u32[]{:S(2)}) collective-permute-start(bf16[2,1024,128]{2,1,0:T(8,128)(2,1)S(1)} %constant_dynamic-update-slice_fusion.10.refs_4_.refs_6_), channel_id=1, source_target_pairs={{0,8},{8,0},{16,24},{24,16},{1,9},{9,1},{17,25},{25,17},{2,10},{10... | collective-permute-start | bytes 1572872 | tf_op jit(solution)/shard_map/ppermute | solution.py:294
  117.9 21.7 %collective-permute-start.27 = (bf16[2,1024,128]{2,1,0:T(8,128)(2,1)S(1)}, bf16[2,1024,128]{2,1,0:T(8,128)(2,1)S(1)}, u32[]{:S(2)}, u32[]{:S(2)}) collective-permute-start(bf16[2,1024,128]{2,1,0:T(8,128)(2,1)S(1)} %constant_dynamic-update-slice_fusion.12.refs_0_.refs_1_), channel_id=1, source_target_pairs={{0,16},{8,24},{16,0},{24,8},{1,17},{9,25},{17,1},{25,9},{2,18},{10... | collective-permute-start | bytes 1572872 | tf_op jit(solution)/shard_map/ppermute | solution.py:294
  118.4 22.7 %collective-permute-start.28 = (bf16[2,1024,128]{2,1,0:T(8,128)(2,1)S(1)}, bf16[2,1024,128]{2,1,0:T(8,128)(2,1)S(1)}, u32[]{:S(2)}, u32[]{:S(2)}) collective-permute-start(bf16[2,1024,128]{2,1,0:T(8,128)(2,1)S(1)} %constant_dynamic-update-slice_fusion.14.refs_4_.refs_6_), channel_id=1, source_target_pairs={{0,8},{8,0},{16,24},{24,16},{1,9},{9,1},{17,25},{25,17},{2,10},{10... | collective-permute-start | bytes 1572872 | tf_op jit(solution)/shard_map/ppermute | solution.py:294
  (38 other events, 248.1 us)

commit v2 on v1

--- a/solution.py
+++ b/solution.py
@@ -178,6 +178,33 @@
     )(tokens, attended, out, up, down)
 
 
+def split_join_kernel(level_ref, weight_ref, skip_ref, out_ref):
+    width = out_ref.shape[1] // 4
+    for i in range(4):
+        columns = slice(i * width, (i + 1) * width)
+        expanded = jnp.dot(
+            level_ref[...], weight_ref[:, columns], preferred_element_type=jnp.float32
+        )
+        joined = skip_ref[:, columns].astype(jnp.float32) + layer_norm(expanded)
+        out_ref[:, columns] = joined.astype(jnp.bfloat16)
+
+
+def split_join(level, weight, merged):
+    whole = pl.BlockSpec(memory_space=pltpu.VMEM)
+    return pl.pallas_call(
+        split_join_kernel,
+        out_shape=jax.ShapeDtypeStruct(merged.shape, jnp.bfloat16),
+        in_specs=[whole] * 3,
+        out_specs=whole,
+        compiler_params=pltpu.CompilerParams(vmem_limit_bytes=32 * 2**20),
+        cost_estimate=pl.CostEstimate(
+            flops=2 * merged.shape[0] * weight.shape[0] * weight.shape[1],
+            bytes_accessed=2 * weight.shape[0] * weight.shape[1],
+            transcendentals=0,
+        ),
+    )(level, weight, merged)
+
+
 def coarse_attend_kernel(x_ref, qkv_ref, rows_ref, a0_ref, a1_ref, b0_ref, b1_ref, own_ref, peer_ref, sum_ref):
     lat = lax.axis_index("lat")
     count, width = x_ref.shape
@@ -470,13 +497,12 @@
             .transpose(0, 2, 1, 3, 4)
             .reshape(coarse_rows * coarse_cols, -1)
         )
-    expanded = project(level_state, split_weight)
-    expanded = (
-        expanded.reshape(wins[0], wins[3], WH, WW, 2, 2, -1)
+    joined = split_join(level_state, split_weight, merged)
+    return (
+        joined.reshape(wins[0], wins[3], WH, WW, 2, 2, -1)
         .transpose(0, 2, 4, 1, 3, 5, 6)
-        .reshape(band_rows, band_cols, -1)
-    )
-    return (skip_tokens.astype(jnp.float32) + layer_norm(expanded)).astype(jnp.bfloat16)
+        .reshape(tokens.shape)
+    )
 
 
 def solution(mesh):

time: 157 us -> 148 us (0.943)
  other arithmetic: 13 us -> 5.6 us
  waiting for transfers between devices: 35.3 us -> 42.5 us
  local copies, waits for them, and re-layouts: 29.4 us -> 22.8 us
  starting transfers between devices: 50 us -> 47.8 us
  matrix products: 3.68 us -> 1.97 us
    ppermute x20, waiting for transfers between devices: 27.8 us -> 31.6 us  [swapped(): lax.ppermute(block, axis, [(i, i ^ bit) for i in range(lax.axis_size(axis...]
    ppermute x20, starting transfers between devices: 28.8 us -> 25.7 us  [swapped(): lax.ppermute(block, axis, [(i, i ^ bit) for i in range(lax.axis_size(axis...]
    slice x6, local copies, waits for them, and re-layouts: 6.31 us -> 4.16 us  [first_swap(): b = jnp.stack([one[1] for one in got])]
    reduce_sum x5 -> x4, other arithmetic: 3.2 us -> 1.07 us  [layer_norm(): spread = jnp.mean(centred * centred, axis=-1, keepdims=True)]
    ppermute x4, waiting for transfers between devices: 4.81 us -> 6.67 us  [shifted_2(): return lax.ppermute(block, axis, route)]
    dot_general x3 -> x2, matrix products: 3.68 us -> 1.97 us  [project(): result = jnp.dot(flattened, matrix, preferred_element_type=jnp.float32)]
    concatenate x2, other arithmetic: 1.85 us -> 0.16 us  [per_device(): shifted = jnp.concatenate([tokens[SH:], below_rows], axis=0)]
    reshape x2, local copies, waits for them, and re-layouts: 3.09 us -> 1.47 us  [the longest x1 1.04 us: per_device(): return joined.reshape(wins[0], wins[3], WH, WW, 2, 2, -1).transpose(0, 2,...]
  transfers between devices with their start and end apart: 30 -> 30, of which waited for: 13 -> 14; matrix products, arithmetic and copies ran while one was open for 20% -> 16% of each run, Pallas kernels for 14% -> 15%
where the time goes in v2:
time: 148 us; the launch traced here: 146 us
  starting transfers between devices  47.8 us (32%)
  waiting for transfers between devices  42.5 us (29%)
  Pallas kernels  24.5 us (17%)
  local copies, waits for them, and re-layouts  22.8 us (15%)
  other arithmetic  5.6 us (4%)
  matrix products  1.97 us (1%)
    ppermute x20, waiting for transfers between devices, swapped(): lax.ppermute(block, axis, [(i, i ^ bit) for i in range(lax.axis_size(axis...  31.6 us
    ppermute x20, starting transfers between devices, swapped(): lax.ppermute(block, axis, [(i, i ^ bit) for i in range(lax.axis_size(axis...  25.7 us
    ppermute x4, starting transfers between devices, shifted_2(): return lax.ppermute(block, axis, route)  11.1 us
    ppermute x6, starting transfers between devices, along_lon(): lax.ppermute(both, 'lon', [(i, (i + shift) % lons) for i in range(lons)])  11 us
    pallas_call x1, Pallas kernels, fine_attend(): pl.pallas_call(functools.partial(fine_kernel, width // (3 * HD)), out_sha...  8.45 us
    pallas_call x1, Pallas kernels, coarse_attend(): pl.pallas_call(coarse_attend_kernel, out_shape=(jax.ShapeDtypeStruct((cou...  6.95 us
    ppermute x4, waiting for transfers between devices, shifted_2(): return lax.ppermute(block, axis, route)  6.67 us
    pallas_call x1, Pallas kernels, fine_mlp(): pl.pallas_call(fine_mlp_kernel, out_shape=jax.ShapeDtypeStruct((count, wi...  4.56 us
  transfers between devices with their start and end apart: 30, of which 14 were waited for; matrix products, arithmetic and copies ran while one was open for 16% of the time, Pallas kernels for 15%

profile of v2, /device:TPU:1, one launch (start us, length us, event | category | flops | bytes accessed | tf_op | source)
XLA Modules:
  0.0 146.0 jit_solution(12353521319141944818)
XLA Ops:
  1.1 3.0 %collective-permute-start = (bf16[3,48,512]{2,1,0:T(8,128)(2,1)S(1)}, bf16[3,48,512]{2,1,0:T(8,128)(2,1)S(1)}, u32[]{:S(2)}, u32[]{:S(2)}) collective-permute-start(bf16[3,48,512]{2,1,0:T(8,128)(2,1)S(1)} %slice.77), channel_id=1, source_target_pairs={{8,0},{16,8},{24,16},{0,24},{9,1},{17,9},{25,17},{1,25},{10,2},{18... | collective-permute-start | bytes 442376 | tf_op jit(solution)/shard_map/ppermute | solution.py:20
  6.2 1.9 %constant_dynamic-slice_fusion.1 = (bf16[1024,128]{1,0:T(8,128)(2,1)}, bf16[1024,128]{1,0:T(8,128)(2,1)}) fusion(bf16[1024,512]{1,0:T(8,128)(2,1)} %refs_1_.1, s32[]{:T(128)S(6)} %select_n.21, bf16[1024,512]{1,0:T(8,128)(2,1)} %refs_0_.1), kind=kLoop, calls=%fused_computation.69 | loop fusion | bytes 1048580 | tf_op jit(solution)/shard_map/dynamic_slice | solution.py:352
  9.3 3.3 %collective-permute-done.1 = bf16[12,6,512]{2,1,0:T(8,128)(2,1)S(1)} collective-permute-done((bf16[12,6,512]{2,1,0:T(8,128)(2,1)S(1)}, bf16[12,6,512]{2,1,0:T(8,128)(2,1)S(1)}, u32[]{:S(2)}, u32[]{:S(2)}) %collective-permute-start.1) | collective-permute-done | bytes 73760 | tf_op jit(solution)/shard_map/ppermute | solution.py:20
  14.7 3.7 %collective-permute-start.3 = (bf16[2,512,128]{2,1,0:T(8,128)(2,1)}, bf16[2,512,128]{2,1,0:T(8,128)(2,1)S(1)}, u32[]{:S(2)}, u32[]{:S(2)}) collective-permute-start(bf16[2,512,128]{2,1,0:T(8,128)(2,1)} %pad_maximum_fusion.8), channel_id=1, source_target_pairs={{0,4},{1,5},{2,6},{3,7},{4,0},{5,1},{6,2},{7,3},{8,12},{9,13},{10,... | collective-permute-start | bytes 786440 | tf_op jit(solution)/shard_map/ppermute | solution.py:328
  21.7 1.4 reshape.85
  25.1 8.4 %shard_map.109 = bf16[8,72,512]{2,1,0:T(8,128)(2,1)S(1)} custom-call(bf16[8,72,1536]{2,1,0:T(8,128)(2,1)S(1)} %convolution_convert_fusion.qkv_ref, f32[2,72,72]{2,1,0:T(8,128)S(1)} %compare_select_fusion.bias_ref), custom_call_target="tpu_custom_call" | custom-call | flops 84934656 | bytes 2654208 | tf_op jit(solution)/shard_map/pallas_call | solution.py:113
  33.6 2.7 %collective-permute-done.3 = bf16[2,512,128]{2,1,0:T(8,128)(2,1)S(1)} collective-permute-done((bf16[2,512,128]{2,1,0:T(8,128)(2,1)}, bf16[2,512,128]{2,1,0:T(8,128)(2,1)S(1)}, u32[]{:S(2)}, u32[]{:S(2)}) %collective-permute-start.3) | collective-permute-done | bytes 262176 | tf_op jit(solution)/shard_map/ppermute | solution.py:328
  43.8 1.6 %collective-permute-done.5 = bf16[3,48,512]{2,1,0:T(8,128)(2,1)S(1)} collective-permute-done((bf16[3,48,512]{2,1,0:T(8,128)(2,1)S(1)}, bf16[3,48,512]{2,1,0:T(8,128)(2,1)S(1)}, u32[]{:S(2)}, u32[]{:S(2)}) %collective-permute-start.5) | collective-permute-done | bytes 147488 | tf_op jit(solution)/shard_map/ppermute | solution.py:20
  45.4 6.3 %collective-permute-start.6 = (bf16[12,6,512]{2,1,0:T(8,128)(2,1)S(1)}, bf16[12,6,512]{2,1,0:T(8,128)(2,1)S(1)}, u32[]{:S(2)}, u32[]{:S(2)}) collective-permute-start(bf16[12,6,512]{2,1,0:T(8,128)(2,1)S(1)} %pad_maximum_fusion.11), channel_id=1, source_target_pairs={{7,0},{0,1},{1,2},{2,3},{3,4},{4,5},{5,6},{6,7},{15,8},{8,9},{9,10... | collective-permute-start | bytes 221192 | tf_op jit(solution)/shard_map/ppermute | solution.py:20
  51.9 1.7 %collective-permute-done.6 = bf16[12,6,512]{2,1,0:T(8,128)(2,1)S(1)} collective-permute-done((bf16[12,6,512]{2,1,0:T(8,128)(2,1)S(1)}, bf16[12,6,512]{2,1,0:T(8,128)(2,1)S(1)}, u32[]{:S(2)}, u32[]{:S(2)}) %collective-permute-start.6) | collective-permute-done | bytes 73760 | tf_op jit(solution)/shard_map/ppermute | solution.py:20
  54.9 4.1 %collective-permute-start.12 = (bf16[2,1024,128]{2,1,0:T(8,128)(2,1)}, bf16[2,1024,128]{2,1,0:T(8,128)(2,1)}, u32[]{:S(2)}, u32[]{:S(2)}) collective-permute-start(bf16[2,1024,128]{2,1,0:T(8,128)(2,1)} %pad_maximum_fusion.5), channel_id=1, source_target_pairs={{0,6},{1,7},{2,0},{3,1},{4,2},{5,3},{6,4},{7,5},{8,14},{9,15},{10,... | collective-permute-start | bytes 1572872 | tf_op jit(solution)/shard_map/ppermute | solution.py:328
  59.0 1.8 %collective-permute-start.18 = (bf16[2,1024,128]{2,1,0:T(8,128)(2,1)}, bf16[2,1024,128]{2,1,0:T(8,128)(2,1)}, u32[]{:S(2)}, u32[]{:S(2)}) collective-permute-start(bf16[2,1024,128]{2,1,0:T(8,128)(2,1)} %pad_maximum_fusion.5), channel_id=1, source_target_pairs={{0,4},{1,5},{2,6},{3,7},{4,0},{5,1},{6,2},{7,3},{8,12},{9,13},{10,... | collective-permute-start | bytes 1572872 | tf_op jit(solution)/shard_map/ppermute | solution.py:328
  60.8 4.6 %shard_map.110 = bf16[576,512]{1,0:T(8,128)(2,1)S(1)} custom-call(bf16[576,512]{1,0:T(8,128)(2,1)S(1)} %bitcast.23, bf16[576,512]{1,0:T(8,128)(2,1)S(1)} %bitcast.22, bf16[512,512]{1,0:T(8,128)(2,1)S(1)} %copy-done.9, bf16[512,2048]{1,0:T(8,128)(2,1)S(1)} %copy-done.7, bf16[2048,512]{1,0:T(8,128)(2,1)S(1)} %copy-done.8), custom_call_target="tpu_custom_call" | custom-call | flops 2717908992 | bytes 4718592 | tf_op jit(solution)/shard_map/pallas_call | solution.py:156
  69.7 1.8 %constant_dynamic-update-slice_fusion.2.b0_ref = bf16[6,512,128]{2,1,0:T(8,128)(2,1)} fusion(bf16[6,512,128]{2,1,0:T(8,128)(2,1)} %constant_dynamic-update-slice_fusion.3, bf16[3,512,128]{2,1,0:T(8,128)(2,1)} %copy-done.23), kind=kLoop, calls=%fused_computation.48 | loop fusion | bytes 786432 | tf_op jit(solution)/shard_map/concatenate | solution.py:340
  74.7 1.6 %collective-permute-done.12 = bf16[2,1024,128]{2,1,0:T(8,128)(2,1)} collective-permute-done((bf16[2,1024,128]{2,1,0:T(8,128)(2,1)}, bf16[2,1024,128]{2,1,0:T(8,128)(2,1)}, u32[]{:S(2)}, u32[]{:S(2)}) %collective-permute-start.12) | collective-permute-done | bytes 524320 | tf_op jit(solution)/shard_map/ppermute | solution.py:328
  76.8 3.4 %collective-permute-start.13 = (bf16[144,1024]{1,0:T(8,128)(2,1)S(1)}, bf16[144,1024]{1,0:T(8,128)(2,1)S(1)}, u32[]{:S(2)}, u32[]{:S(2)}) collective-permute-start(bf16[144,1024]{1,0:T(8,128)(2,1)S(1)} %multiply_convert_fusion.1), channel_id=1, source_target_pairs={{0,1},{1,0},{2,3},{3,2},{4,5},{5,4},{6,7},{7,6},{8,9},{9,8},{10,11... | collective-permute-start | bytes 884744 | tf_op jit(solution)/shard_map/ppermute | solution.py:321
  83.7 6.0 %collective-permute-done.14.a1_ref = bf16[6,512,128]{2,1,0:T(8,128)(2,1)} collective-permute-done((bf16[6,512,128]{2,1,0:T(8,128)(2,1)S(1)}, bf16[6,512,128]{2,1,0:T(8,128)(2,1)}, u32[]{:S(2)}, u32[]{:S(2)}) %collective-permute-start.14) | collective-permute-done | bytes 786464 | tf_op jit(solution)/shard_map/ppermute | solution.py:321
  91.6 7.0 %shard_map.111 = (f32[144,1024]{1,0:T(8,128)S(1)}, bf16[144,1024]{1,0:T(8,128)(2,1)S(1)}) custom-call(bf16[288,1024]{1,0:T(8,128)(2,1)S(1)} %pad_maximum_fusion.2.x_ref, bf16[1024,384]{1,0:T(8,128)(2,1)S(1)} %copy-done.4, bf16[1024,128]{1,0:T(8,128)(2,1)S(1)} %copy-done.6, bf16[6,512,128]{2,1,0:T(8,128)(2,1)S(1)} %constant_dynamic-update-slice_fusion.a0_ref, ...), custom_call_target="tpu_custom_call" | custom-call | flops 1207959552 | bytes 4194304 | tf_op jit(solution)/shard_map/pallas_call | solution.py:253
  98.6 6.9 %collective-permute-start.19 = (bf16[144,1024]{1,0:T(8,128)(2,1)S(1)}, bf16[144,1024]{1,0:T(8,128)(2,1)S(1)}, u32[]{:S(2)}, u32[]{:S(2)}) collective-permute-start(bf16[144,1024]{1,0:T(8,128)(2,1)S(1)} %get-tuple-element.70), channel_id=1, source_target_pairs={{0,1},{1,0},{2,3},{3,2},{4,5},{5,4},{6,7},{7,6},{8,9},{9,8},{10,11... | collective-permute-start | bytes 884744 | tf_op jit(solution)/shard_map/ppermute | solution.py:321
  111.3 3.7 %collective-permute-done.21 = bf16[1,1024,128]{2,1,0:T(8,128)(2,1)S(1)} collective-permute-done((bf16[1,1024,128]{2,1,0:T(8,128)(2,1)S(1)}, bf16[1,1024,128]{2,1,0:T(8,128)(2,1)S(1)}, u32[]{:S(2)}, u32[]{:S(2)}) %collective-permute-start.21) | collective-permute-done | bytes 262176 | tf_op jit(solution)/shard_map/ppermute | solution.py:321
  119.3 6.9 %collective-permute-done.25.refs_2_.refs_3_ = bf16[2,1024,128]{2,1,0:T(8,128)(2,1)S(1)} collective-permute-done((bf16[2,1024,128]{2,1,0:T(8,128)(2,1)S(1)}, bf16[2,1024,128]{2,1,0:T(8,128)(2,1)S(1)}, u32[]{:S(2)}, u32[]{:S(2)}) %collective-permute-start.25) | collective-permute-done | bytes 524320 | tf_op jit(solution)/shard_map/ppermute | solution.py:321
  126.2 1.4 collective-permute-done.26.refs_5_.refs_7_
  128.6 8.9 %collective-permute-done.27.refs_2_.refs_3_ = bf16[2,1024,128]{2,1,0:T(8,128)(2,1)S(1)} collective-permute-done((bf16[2,1024,128]{2,1,0:T(8,128)(2,1)S(1)}, bf16[2,1024,128]{2,1,0:T(8,128)(2,1)S(1)}, u32[]{:S(2)}, u32[]{:S(2)}) %collective-permute-start.27) | collective-permute-done | bytes 524320 | tf_op jit(solution)/shard_map/ppermute | solution.py:321
  139.8 1.8 %collective-permute-start.29 = (bf16[144,1024]{1,0:T(8,128)(2,1)S(1)}, bf16[144,1024]{1,0:T(8,128)(2,1)S(1)}, u32[]{:S(2)}, u32[]{:S(2)}) collective-permute-start(bf16[144,1024]{1,0:T(8,128)(2,1)S(1)} %slice.115), channel_id=1, source_target_pairs={{0,1},{1,0},{2,3},{3,2},{4,5},{5,4},{6,7},{7,6},{8,9},{9,8},{10,11... | collective-permute-start | bytes 884744 | tf_op jit(solution)/shard_map/ppermute | solution.py:321
  (189 shorter events, 51.0 us)
Async XLA Ops:
  1.1 7.1 %collective-permute-start = (bf16[3,48,512]{2,1,0:T(8,128)(2,1)S(1)}, bf16[3,48,512]{2,1,0:T(8,128)(2,1)S(1)}, u32[]{:S(2)}, u32[]{:S(2)}) collective-permute-start(bf16[3,48,512]{2,1,0:T(8,128)(2,1)S(1)} %slice.77), channel_id=1, source_target_pairs={{8,0},{16,8},{24,16},{0,24},{9,1},{17,9},{25,17},{1,25},{10,2},{18... | collective-permute-start | bytes 442376 | tf_op jit(solution)/shard_map/ppermute | solution.py:20
  13.4 20.2 %collective-permute-start.2 = (bf16[2,512,128]{2,1,0:T(8,128)(2,1)}, bf16[2,512,128]{2,1,0:T(8,128)(2,1)S(1)}, u32[]{:S(2)}, u32[]{:S(2)}) collective-permute-start(bf16[2,512,128]{2,1,0:T(8,128)(2,1)} %pad_maximum_fusion.8), channel_id=1, source_target_pairs={{0,2},{1,3},{2,4},{3,5},{4,6},{5,7},{6,0},{7,1},{8,10},{9,11},{10,... | collective-permute-start | bytes 786440 | tf_op jit(solution)/shard_map/ppermute | solution.py:328
  14.7 21.5 %collective-permute-start.3 = (bf16[2,512,128]{2,1,0:T(8,128)(2,1)}, bf16[2,512,128]{2,1,0:T(8,128)(2,1)S(1)}, u32[]{:S(2)}, u32[]{:S(2)}) collective-permute-start(bf16[2,512,128]{2,1,0:T(8,128)(2,1)} %pad_maximum_fusion.8), channel_id=1, source_target_pairs={{0,4},{1,5},{2,6},{3,7},{4,0},{5,1},{6,2},{7,3},{8,12},{9,13},{10,... | collective-permute-start | bytes 786440 | tf_op jit(solution)/shard_map/ppermute | solution.py:328
  18.4 17.8 %collective-permute-start.4 = (bf16[2,512,128]{2,1,0:T(8,128)(2,1)}, bf16[2,512,128]{2,1,0:T(8,128)(2,1)}, u32[]{:S(2)}, u32[]{:S(2)}) collective-permute-start(bf16[2,512,128]{2,1,0:T(8,128)(2,1)} %pad_maximum_fusion.8), channel_id=1, source_target_pairs={{0,6},{1,7},{2,0},{3,1},{4,2},{5,3},{6,4},{7,5},{8,14},{9,15},{10,... | collective-permute-start | bytes 786440 | tf_op jit(solution)/shard_map/ppermute | solution.py:328
  41.6 12.3 %collective-permute-start.7 = (bf16[3,512,128]{2,1,0:T(8,128)(2,1)S(1)}, bf16[3,512,128]{2,1,0:T(8,128)(2,1)S(1)}, u32[]{:S(2)}, u32[]{:S(2)}) collective-permute-start(bf16[3,512,128]{2,1,0:T(8,128)(2,1)S(1)} %pad_maximum_fusion.6), channel_id=1, source_target_pairs={{0,8},{8,0},{16,24},{24,16},{1,9},{9,1},{17,25},{25,17},{2,10},{10... | collective-permute-start | bytes 1179656 | tf_op jit(solution)/shard_map/ppermute | solution.py:321
  42.5 11.4 %collective-permute-start.8 = (bf16[3,512,128]{2,1,0:T(8,128)(2,1)S(1)}, bf16[3,512,128]{2,1,0:T(8,128)(2,1)S(1)}, u32[]{:S(2)}, u32[]{:S(2)}) collective-permute-start(bf16[3,512,128]{2,1,0:T(8,128)(2,1)S(1)} %pad_maximum_fusion.7), channel_id=1, source_target_pairs={{0,16},{8,24},{16,0},{24,8},{1,17},{9,25},{17,1},{25,9},{2,18},{10... | collective-permute-start | bytes 1179656 | tf_op jit(solution)/shard_map/ppermute | solution.py:321
  45.4 8.2 %collective-permute-start.6 = (bf16[12,6,512]{2,1,0:T(8,128)(2,1)S(1)}, bf16[12,6,512]{2,1,0:T(8,128)(2,1)S(1)}, u32[]{:S(2)}, u32[]{:S(2)}) collective-permute-start(bf16[12,6,512]{2,1,0:T(8,128)(2,1)S(1)} %pad_maximum_fusion.11), channel_id=1, source_target_pairs={{7,0},{0,1},{1,2},{2,3},{3,4},{4,5},{5,6},{6,7},{15,8},{8,9},{9,10... | collective-permute-start | bytes 221192 | tf_op jit(solution)/shard_map/ppermute | solution.py:20
  51.9 13.5 %collective-permute-start.9 = (bf16[2,1024,128]{2,1,0:T(8,128)(2,1)S(1)}, bf16[2,1024,128]{2,1,0:T(8,128)(2,1)S(1)}, u32[]{:S(2)}, u32[]{:S(2)}) collective-permute-start(bf16[2,1024,128]{2,1,0:T(8,128)(2,1)S(1)} %pad_maximum_fusion.4), channel_id=1, source_target_pairs={{0,2},{1,3},{2,4},{3,5},{4,6},{5,7},{6,0},{7,1},{8,10},{9,11},{10,... | collective-permute-start | bytes 1572872 | tf_op jit(solution)/shard_map/ppermute | solution.py:328
  54.9 21.4 %collective-permute-start.12 = (bf16[2,1024,128]{2,1,0:T(8,128)(2,1)}, bf16[2,1024,128]{2,1,0:T(8,128)(2,1)}, u32[]{:S(2)}, u32[]{:S(2)}) collective-permute-start(bf16[2,1024,128]{2,1,0:T(8,128)(2,1)} %pad_maximum_fusion.5), channel_id=1, source_target_pairs={{0,6},{1,7},{2,0},{3,1},{4,2},{5,3},{6,4},{7,5},{8,14},{9,15},{10,... | collective-permute-start | bytes 1572872 | tf_op jit(solution)/shard_map/ppermute | solution.py:328
  59.0 39.6 %collective-permute-start.18 = (bf16[2,1024,128]{2,1,0:T(8,128)(2,1)}, bf16[2,1024,128]{2,1,0:T(8,128)(2,1)}, u32[]{:S(2)}, u32[]{:S(2)}) collective-permute-start(bf16[2,1024,128]{2,1,0:T(8,128)(2,1)} %pad_maximum_fusion.5), channel_id=1, source_target_pairs={{0,4},{1,5},{2,6},{3,7},{4,0},{5,1},{6,2},{7,3},{8,12},{9,13},{10,... | collective-permute-start | bytes 1572872 | tf_op jit(solution)/shard_map/ppermute | solution.py:328
  67.3 6.6 %collective-permute-start.11 = (bf16[1,1024,128]{2,1,0:T(8,128)(2,1)S(1)}, bf16[1,1024,128]{2,1,0:T(8,128)(2,1)S(1)}, u32[]{:S(2)}, u32[]{:S(2)}) collective-permute-start(bf16[1,1024,128]{2,1,0:T(8,128)(2,1)S(1)} %get-tuple-element.75), channel_id=1, source_target_pairs={{0,16},{8,24},{16,0},{24,8},{1,17},{9,25},{17,1},{25,9},{2,18},{10... | collective-permute-start | bytes 786440 | tf_op jit(solution)/shard_map/ppermute | solution.py:321
  68.6 21.1 %collective-permute-start.14 = (bf16[6,512,128]{2,1,0:T(8,128)(2,1)S(1)}, bf16[6,512,128]{2,1,0:T(8,128)(2,1)}, u32[]{:S(2)}, u32[]{:S(2)}) collective-permute-start(bf16[6,512,128]{2,1,0:T(8,128)(2,1)S(1)} %constant_dynamic-update-slice_fusion.a0_ref), channel_id=1, source_target_pairs={{0,16},{8,24},{16,0},{24,8},{1,17},{9,25},{17,1},{25,9},{2,18},{10... | collective-permute-start | bytes 2359304 | tf_op jit(solution)/shard_map/ppermute | solution.py:321
  73.3 17.4 %collective-permute-start.15 = (bf16[6,512,128]{2,1,0:T(8,128)(2,1)}, bf16[6,512,128]{2,1,0:T(8,128)(2,1)}, u32[]{:S(2)}, u32[]{:S(2)}) collective-permute-start(bf16[6,512,128]{2,1,0:T(8,128)(2,1)} %constant_dynamic-update-slice_fusion.2.b0_ref), channel_id=1, source_target_pairs={{0,8},{8,0},{16,24},{24,16},{1,9},{9,1},{17,25},{25,17},{2,10},{10... | collective-permute-start | bytes 2359304 | tf_op jit(solution)/shard_map/ppermute | solution.py:321
  81.3 17.3 %collective-permute-start.16 = (bf16[1,1024,128]{2,1,0:T(8,128)(2,1)S(1)}, bf16[1,1024,128]{2,1,0:T(8,128)(2,1)S(1)}, u32[]{:S(2)}, u32[]{:S(2)}) collective-permute-start(bf16[1,1024,128]{2,1,0:T(8,128)(2,1)S(1)} %get-tuple-element.77), channel_id=1, source_target_pairs={{0,8},{8,0},{16,24},{24,16},{1,9},{9,1},{17,25},{25,17},{2,10},{10... | collective-permute-start | bytes 786440 | tf_op jit(solution)/shard_map/ppermute | solution.py:321
  82.7 15.9 %collective-permute-start.17 = (bf16[1,1024,128]{2,1,0:T(8,128)(2,1)S(1)}, bf16[1,1024,128]{2,1,0:T(8,128)(2,1)S(1)}, u32[]{:S(2)}, u32[]{:S(2)}) collective-permute-start(bf16[1,1024,128]{2,1,0:T(8,128)(2,1)S(1)} %get-tuple-element.79), channel_id=1, source_target_pairs={{0,16},{8,24},{16,0},{24,8},{1,17},{9,25},{17,1},{25,9},{2,18},{10... | collective-permute-start | bytes 786440 | tf_op jit(solution)/shard_map/ppermute | solution.py:321
  89.7 26.5 %collective-permute-start.23 = (bf16[2,1024,128]{2,1,0:T(8,128)(2,1)S(1)}, bf16[2,1024,128]{2,1,0:T(8,128)(2,1)S(1)}, u32[]{:S(2)}, u32[]{:S(2)}) collective-permute-start(bf16[2,1024,128]{2,1,0:T(8,128)(2,1)S(1)} %constant_dynamic-update-slice_fusion.4.refs_0_.refs_1_), channel_id=1, source_target_pairs={{0,16},{8,24},{16,0},{24,8},{1,17},{9,25},{17,1},{25,9},{2,18},{10... | collective-permute-start | bytes 1572872 | tf_op jit(solution)/shard_map/ppermute | solution.py:321
  90.7 27.7 %collective-permute-start.24 = (bf16[2,1024,128]{2,1,0:T(8,128)(2,1)S(1)}, bf16[2,1024,128]{2,1,0:T(8,128)(2,1)S(1)}, u32[]{:S(2)}, u32[]{:S(2)}) collective-permute-start(bf16[2,1024,128]{2,1,0:T(8,128)(2,1)S(1)} %constant_dynamic-update-slice_fusion.6.refs_4_.refs_6_), channel_id=1, source_target_pairs={{0,8},{8,0},{16,24},{24,16},{1,9},{9,1},{17,25},{25,17},{2,10},{10... | collective-permute-start | bytes 1572872 | tf_op jit(solution)/shard_map/ppermute | solution.py:321
  98.6 9.0 %collective-permute-start.19 = (bf16[144,1024]{1,0:T(8,128)(2,1)S(1)}, bf16[144,1024]{1,0:T(8,128)(2,1)S(1)}, u32[]{:S(2)}, u32[]{:S(2)}) collective-permute-start(bf16[144,1024]{1,0:T(8,128)(2,1)S(1)} %get-tuple-element.70), channel_id=1, source_target_pairs={{0,1},{1,0},{2,3},{3,2},{4,5},{5,4},{6,7},{7,6},{8,9},{9,8},{10,11... | collective-permute-start | bytes 884744 | tf_op jit(solution)/shard_map/ppermute | solution.py:321
  106.6 8.5 %collective-permute-start.21 = (bf16[1,1024,128]{2,1,0:T(8,128)(2,1)S(1)}, bf16[1,1024,128]{2,1,0:T(8,128)(2,1)S(1)}, u32[]{:S(2)}, u32[]{:S(2)}) collective-permute-start(bf16[1,1024,128]{2,1,0:T(8,128)(2,1)S(1)} %get-tuple-element.81), channel_id=1, source_target_pairs={{0,8},{8,0},{16,24},{24,16},{1,9},{9,1},{17,25},{25,17},{2,10},{10... | collective-permute-start | bytes 786440 | tf_op jit(solution)/shard_map/ppermute | solution.py:321
  107.4 8.4 %collective-permute-start.22 = (bf16[1,1024,128]{2,1,0:T(8,128)(2,1)S(1)}, bf16[1,1024,128]{2,1,0:T(8,128)(2,1)S(1)}, u32[]{:S(2)}, u32[]{:S(2)}) collective-permute-start(bf16[1,1024,128]{2,1,0:T(8,128)(2,1)S(1)} %get-tuple-element.83), channel_id=1, source_target_pairs={{0,16},{8,24},{16,0},{24,8},{1,17},{9,25},{17,1},{25,9},{2,18},{10... | collective-permute-start | bytes 786440 | tf_op jit(solution)/shard_map/ppermute | solution.py:321
  110.0 16.2 %collective-permute-start.25 = (bf16[2,1024,128]{2,1,0:T(8,128)(2,1)S(1)}, bf16[2,1024,128]{2,1,0:T(8,128)(2,1)S(1)}, u32[]{:S(2)}, u32[]{:S(2)}) collective-permute-start(bf16[2,1024,128]{2,1,0:T(8,128)(2,1)S(1)} %constant_dynamic-update-slice_fusion.8.refs_0_.refs_1_), channel_id=1, source_target_pairs={{0,16},{8,24},{16,0},{24,8},{1,17},{9,25},{17,1},{25,9},{2,18},{10... | collective-permute-start | bytes 1572872 | tf_op jit(solution)/shard_map/ppermute | solution.py:321
  115.1 12.6 %collective-permute-start.26 = (bf16[2,1024,128]{2,1,0:T(8,128)(2,1)S(1)}, bf16[2,1024,128]{2,1,0:T(8,128)(2,1)S(1)}, u32[]{:S(2)}, u32[]{:S(2)}) collective-permute-start(bf16[2,1024,128]{2,1,0:T(8,128)(2,1)S(1)} %constant_dynamic-update-slice_fusion.10.refs_4_.refs_6_), channel_id=1, source_target_pairs={{0,8},{8,0},{16,24},{24,16},{1,9},{9,1},{17,25},{25,17},{2,10},{10... | collective-permute-start | bytes 1572872 | tf_op jit(solution)/shard_map/ppermute | solution.py:321
  115.9 21.6 %collective-permute-start.27 = (bf16[2,1024,128]{2,1,0:T(8,128)(2,1)S(1)}, bf16[2,1024,128]{2,1,0:T(8,128)(2,1)S(1)}, u32[]{:S(2)}, u32[]{:S(2)}) collective-permute-start(bf16[2,1024,128]{2,1,0:T(8,128)(2,1)S(1)} %constant_dynamic-update-slice_fusion.12.refs_0_.refs_1_), channel_id=1, source_target_pairs={{0,16},{8,24},{16,0},{24,8},{1,17},{9,25},{17,1},{25,9},{2,18},{10... | collective-permute-start | bytes 1572872 | tf_op jit(solution)/shard_map/ppermute | solution.py:321
  116.2 22.7 %collective-permute-start.28 = (bf16[2,1024,128]{2,1,0:T(8,128)(2,1)S(1)}, bf16[2,1024,128]{2,1,0:T(8,128)(2,1)S(1)}, u32[]{:S(2)}, u32[]{:S(2)}) collective-permute-start(bf16[2,1024,128]{2,1,0:T(8,128)(2,1)S(1)} %constant_dynamic-update-slice_fusion.14.refs_4_.refs_6_), channel_id=1, source_target_pairs={{0,8},{8,0},{16,24},{24,16},{1,9},{9,1},{17,25},{25,17},{2,10},{10... | collective-permute-start | bytes 1572872 | tf_op jit(solution)/shard_map/ppermute | solution.py:321
  (37 other events, 213.7 us)
